TPU v7x, 128 devices: a whole 4x4x4 slice. The times are simulated.
128 devices in a mesh: strip: 128 (over z, y, x, core).
Axes of the slice: x: 4, y: 4, z: 4, core: 2. Of those that a mesh axis runs over, the one named last changes fastest.
Arguments:
- density: float32 [65536, 64], P('strip'), may hold values from -6 to 6
- near_blocks: float32 [65536, 6144], P('strip'), may hold values from -0.078125 to 0.078125
- u_far: bfloat16 [65536, 128, 32], P('strip'), may hold values from -0.09375 to 0.09375
- v_far: bfloat16 [65536, 128, 32], P('strip'), may hold values from -0.25 to 0.25
- ranks: int32 [128, 128], replicated, may hold values from 0 to 32, as said below
- near_list: int32 [128, 12], replicated, may hold values from 0 to 127, as said below
- near_count: int32 [128], replicated, may hold values from 6 to 12, as said below
Outputs:
- potential: float32 [65536, 64], P('strip')
Inputs may be any that keep to these rules, and one draw needn't show every extreme that they name: near_list row i holds i first, then near_count[i] - 1 distinct other strips j with |j - i| <= 8; its remaining entries repeat i. `near_count`: both ends are reached. ranks[i, j] is 0 exactly when j is among the first near_count[i] entries of near_list row i, otherwise from 8 to 32; 32 is reached.
All inputs are finite; a program needn't handle non-finite values.
Results may differ from a plain program's by a relative error of at most 0.0027.
Values may be sent and summed in bfloat16 or wider, within the bound.
No kernel may reach another device: no remote copies, remote signals or barrier semaphores. Data moves between devices by JAX's collectives and lax.ppermute only.
A program may use at most 128 MiB of HBM per device.

v0:
```python
import jax
import jax.numpy as jnp
from jax import lax
from jax.sharding import PartitionSpec as P

WINDOW = 8


def shifted(value, axis, steps):
    count = lax.axis_size(axis)
    initial, last = (max(0, -steps), min(count, count - steps))
    return lax.ppermute(value, axis, [(source, source + steps) for source in range(initial, last)])


def body(density, near_blocks, u_far, v_far, ranks, near_list, near_count):
    strips = lax.axis_size("strip")
    own_index = lax.axis_index("strip")
    strip_rows = density.shape[0]
    sides = density.shape[1]
    slot_total = near_list.shape[1]
    rank_max = u_far.shape[2]
    picks = lax.dynamic_index_in_dim(near_list, own_index, 0, keepdims=False)
    count = lax.dynamic_index_in_dim(near_count, own_index, 0, keepdims=False)
    live = jnp.arange(slot_total, dtype=jnp.int32) < count
    source_bf = density.astype(jnp.bfloat16)
    projected = jnp.einsum("mik,mr->ikr", v_far, source_bf, preferred_element_type=jnp.float32)
    rank_column = lax.dynamic_index_in_dim(ranks, own_index, 1, keepdims=False)
    keep = jnp.arange(rank_max, dtype=jnp.int32)[None, :] < rank_column[:, None]
    outgoing = (
        jnp.where(keep[:, :, None], projected, 0.0)
        .astype(jnp.bfloat16)
        .reshape(strips, rank_max * sides)
    )
    incoming = lax.all_to_all(outgoing, "strip", split_axis=0, concat_axis=0, tiled=True)
    far_field = jnp.dot(
        u_far.reshape(strip_rows, strips * rank_max),
        incoming.reshape(strips * rank_max, sides),
        preferred_element_type=jnp.float32,
    )
    pieces = []
    for offset in range(-WINDOW, WINDOW + 1):
        if offset == 0:
            pieces.append(density)
        else:
            pieces.append(shifted(density, "strip", -offset))
    stacked = jnp.stack(pieces)
    gathered = jnp.take(stacked, picks - own_index + WINDOW, axis=0)
    gathered = jnp.where(live[:, None, None], gathered, 0.0)
    near_field = jnp.dot(
        near_blocks,
        gathered.reshape(slot_total * strip_rows, sides),
        precision=lax.Precision.HIGHEST,
        preferred_element_type=jnp.float32,
    )
    return near_field + far_field


def solution(mesh):
    return jax.shard_map(
        body,
        mesh=mesh,
        in_specs=(
            P("strip", None),
            P("strip", None),
            P("strip", None, None),
            P("strip", None, None),
            P(),
            P(),
            P(),
        ),
        out_specs=P("strip", None),
        check_vma=False,
    )
```

profile of v0, /device:TPU:59, one launch (start us, length us, event | category | flops | bytes accessed | tf_op | source)
XLA Modules:
  0.0 126.6 jit_solution(761987937649776767)
XLA Ops:
  0.0 3.3 %collective-permute-start = (f32[512,64]{0,1:T(8,128)}, f32[512,64]{0,1:T(8,128)S(1)}, u32[]{:S(2)}, u32[]{:S(2)}) collective-permute-start(f32[512,64]{0,1:T(8,128)} %param.7), channel_id=1, source_target_pairs={{0,8},{1,9},{2,10},{3,11},{4,12},{5,13},{6,14},{7,15},{8,16},{9,17... | collective-permute-start | bytes 393224 | tf_op jit(solution)/shard_map/ppermute | solution.py:12
  3.3 4.0 %collective-permute-start.1 = (f32[512,64]{0,1:T(8,128)}, f32[512,64]{0,1:T(8,128)S(1)}, u32[]{:S(2)}, u32[]{:S(2)}) collective-permute-start(f32[512,64]{0,1:T(8,128)} %param.7), channel_id=1, source_target_pairs={{0,7},{1,8},{2,9},{3,10},{4,11},{5,12},{6,13},{7,14},{8,15},{9,16}... | collective-permute-start | bytes 393224 | tf_op jit(solution)/shard_map/ppermute | solution.py:12
  7.4 3.2 %collective-permute-start.2 = (f32[512,64]{0,1:T(8,128)}, f32[512,64]{0,1:T(8,128)S(1)}, u32[]{:S(2)}, u32[]{:S(2)}) collective-permute-start(f32[512,64]{0,1:T(8,128)} %param.7), channel_id=1, source_target_pairs={{0,6},{1,7},{2,8},{3,9},{4,10},{5,11},{6,12},{7,13},{8,14},{9,15},... | collective-permute-start | bytes 393224 | tf_op jit(solution)/shard_map/ppermute | solution.py:12
  10.6 4.4 %collective-permute-start.3 = (f32[512,64]{0,1:T(8,128)}, f32[512,64]{0,1:T(8,128)S(1)}, u32[]{:S(2)}, u32[]{:S(2)}) collective-permute-start(f32[512,64]{0,1:T(8,128)} %param.7), channel_id=1, source_target_pairs={{0,5},{1,6},{2,7},{3,8},{4,9},{5,10},{6,11},{7,12},{8,13},{9,14},{... | collective-permute-start | bytes 393224 | tf_op jit(solution)/shard_map/ppermute | solution.py:12
  15.0 2.3 %collective-permute-start.4 = (f32[512,64]{0,1:T(8,128)}, f32[512,64]{0,1:T(8,128)S(1)}, u32[]{:S(2)}, u32[]{:S(2)}) collective-permute-start(f32[512,64]{0,1:T(8,128)} %param.7), channel_id=1, source_target_pairs={{0,4},{1,5},{2,6},{3,7},{4,8},{5,9},{6,10},{7,11},{8,12},{9,13},{1... | collective-permute-start | bytes 393224 | tf_op jit(solution)/shard_map/ppermute | solution.py:12
  17.4 3.7 %fusion.8 = bf16[128,32,64]{0,2,1:T(8,128)(2,1)S(1)} fusion(bf16[512,128,32]{1,2,0:T(8,128)(2,1)} %param.10, pred[128,32]{0,1:T(8,128)(4,1)S(1)} %iota_compare_fusion, f32[512,64]{0,1:T(8,128)} %param.7), kind=kOutput, calls=%fused_computation.7 | convolution fusion | flops 268992512 | bytes 4853760 | tf_op jit(solution)/shard_map/mik,mr->ikr/dot_general | solution.py:26
  21.7 1.0 reduce.9
  23.0 1.2 reshape.98
  24.1 11.3 %all-to-all-start = ((bf16[128,2,1024]{2,1,0:T(2,128)(2,1)}), bf16[128,2,1024]{2,1,0:T(2,128)(2,1)}, u32[]{:S(2)}, u32[]{:S(2)}) async-start(bf16[128,2,1024]{2,1,0:T(2,128)(2,1)} %reshape.98), calls=%async_computation | async-start | bytes 1048576 | tf_op jit(solution)/shard_map/all_to_all | solution.py:34
  36.9 8.6 %copy.16 = bf16[512,128,32]{0,2,1:T(8,128)(2,1)} copy(bf16[512,128,32]{1,2,0:T(8,128)(2,1)} %param.9) | data formatting | bytes 8388608 | tf_op args[2]
  45.8 4.0 %collective-permute-start.5 = (f32[512,64]{0,1:T(8,128)S(1)}, f32[512,64]{0,1:T(8,128)S(1)}, u32[]{:S(2)}, u32[]{:S(2)}) collective-permute-start(f32[512,64]{0,1:T(8,128)S(1)} %copy-done.1), channel_id=1, source_target_pairs={{0,3},{1,4},{2,5},{3,6},{4,7},{5,8},{6,9},{7,10},{8,11},{9,12},{10... | collective-permute-start | bytes 393224 | tf_op jit(solution)/shard_map/ppermute | solution.py:12
  50.4 2.5 %collective-permute-start.6 = (f32[512,64]{0,1:T(8,128)S(1)}, f32[512,64]{0,1:T(8,128)S(1)}, u32[]{:S(2)}, u32[]{:S(2)}) collective-permute-start(f32[512,64]{0,1:T(8,128)S(1)} %copy-done.1), channel_id=1, source_target_pairs={{0,2},{1,3},{2,4},{3,5},{4,6},{5,7},{6,8},{7,9},{8,10},{9,11},{10,... | collective-permute-start | bytes 393224 | tf_op jit(solution)/shard_map/ppermute | solution.py:12
  53.6 3.1 %collective-permute-start.7 = (f32[512,64]{0,1:T(8,128)S(1)}, f32[512,64]{0,1:T(8,128)S(1)}, u32[]{:S(2)}, u32[]{:S(2)}) collective-permute-start(f32[512,64]{0,1:T(8,128)S(1)} %copy-done.1), channel_id=1, source_target_pairs={{0,1},{1,2},{2,3},{3,4},{4,5},{5,6},{6,7},{7,8},{8,9},{9,10},{10,1... | collective-permute-start | bytes 393224 | tf_op jit(solution)/shard_map/ppermute | solution.py:12
  57.4 1.9 %collective-permute-start.8 = (f32[512,64]{0,1:T(8,128)S(1)}, f32[512,64]{0,1:T(8,128)S(1)}, u32[]{:S(2)}, u32[]{:S(2)}) collective-permute-start(f32[512,64]{0,1:T(8,128)S(1)} %copy-done.1), channel_id=1, source_target_pairs={{1,0},{2,1},{3,2},{4,3},{5,4},{6,5},{7,6},{8,7},{9,8},{10,9},{11,1... | collective-permute-start | bytes 393224 | tf_op jit(solution)/shard_map/ppermute | solution.py:12
  59.3 0.7 bitcast_dynamic-update-slice_fusion.13
  60.0 2.2 %collective-permute-start.9 = (f32[512,64]{0,1:T(8,128)S(1)}, f32[512,64]{0,1:T(8,128)S(1)}, u32[]{:S(2)}, u32[]{:S(2)}) collective-permute-start(f32[512,64]{0,1:T(8,128)S(1)} %copy-done.1), channel_id=1, source_target_pairs={{2,0},{3,1},{4,2},{5,3},{6,4},{7,5},{8,6},{9,7},{10,8},{11,9},{12,... | collective-permute-start | bytes 393224 | tf_op jit(solution)/shard_map/ppermute | solution.py:12
  62.8 5.4 %collective-permute-start.10 = (f32[512,64]{0,1:T(8,128)S(1)}, f32[512,64]{0,1:T(8,128)S(1)}, u32[]{:S(2)}, u32[]{:S(2)}) collective-permute-start(f32[512,64]{0,1:T(8,128)S(1)} %copy-done.1), channel_id=1, source_target_pairs={{3,0},{4,1},{5,2},{6,3},{7,4},{8,5},{9,6},{10,7},{11,8},{12,9},{13... | collective-permute-start | bytes 393224 | tf_op jit(solution)/shard_map/ppermute | solution.py:12
  68.9 1.9 %collective-permute-start.11 = (f32[512,64]{0,1:T(8,128)S(1)}, f32[512,64]{0,1:T(8,128)S(1)}, u32[]{:S(2)}, u32[]{:S(2)}) collective-permute-start(f32[512,64]{0,1:T(8,128)S(1)} %copy-done.1), channel_id=1, source_target_pairs={{4,0},{5,1},{6,2},{7,3},{8,4},{9,5},{10,6},{11,7},{12,8},{13,9},{1... | collective-permute-start | bytes 393224 | tf_op jit(solution)/shard_map/ppermute | solution.py:12
  71.4 5.1 %collective-permute-start.12 = (f32[512,64]{0,1:T(8,128)S(1)}, f32[512,64]{0,1:T(8,128)S(1)}, u32[]{:S(2)}, u32[]{:S(2)}) collective-permute-start(f32[512,64]{0,1:T(8,128)S(1)} %copy-done.1), channel_id=1, source_target_pairs={{5,0},{6,1},{7,2},{8,3},{9,4},{10,5},{11,6},{12,7},{13,8},{14,9},{... | collective-permute-start | bytes 393224 | tf_op jit(solution)/shard_map/ppermute | solution.py:12
  77.2 0.7 bitcast_dynamic-update-slice_fusion.8
  77.9 3.2 %collective-permute-start.13 = (f32[512,64]{0,1:T(8,128)S(1)}, f32[512,64]{0,1:T(8,128)S(1)}, u32[]{:S(2)}, u32[]{:S(2)}) collective-permute-start(f32[512,64]{0,1:T(8,128)S(1)} %copy-done.1), channel_id=1, source_target_pairs={{6,0},{7,1},{8,2},{9,3},{10,4},{11,5},{12,6},{13,7},{14,8},{15,9},... | collective-permute-start | bytes 393224 | tf_op jit(solution)/shard_map/ppermute | solution.py:12
  81.1 0.7 bitcast_dynamic-update-slice_fusion.7
  81.8 5.2 %collective-permute-start.14 = (f32[512,64]{0,1:T(8,128)S(1)}, f32[512,64]{0,1:T(8,128)S(1)}, u32[]{:S(2)}, u32[]{:S(2)}) collective-permute-start(f32[512,64]{0,1:T(8,128)S(1)} %copy-done.1), channel_id=1, source_target_pairs={{7,0},{8,1},{9,2},{10,3},{11,4},{12,5},{13,6},{14,7},{15,8},{16,9}... | collective-permute-start | bytes 393224 | tf_op jit(solution)/shard_map/ppermute | solution.py:12
  87.7 2.3 %collective-permute-start.15 = (f32[512,64]{0,1:T(8,128)S(1)}, f32[512,64]{0,1:T(8,128)S(1)}, u32[]{:S(2)}, u32[]{:S(2)}) collective-permute-start(f32[512,64]{0,1:T(8,128)S(1)} %copy-done.1), channel_id=1, source_target_pairs={{8,0},{9,1},{10,2},{11,3},{12,4},{13,5},{14,6},{15,7},{16,8},{17,9... | collective-permute-start | bytes 393224 | tf_op jit(solution)/shard_map/ppermute | solution.py:12
  93.3 3.7 %collective-permute-done.15 = f32[512,64]{0,1:T(8,128)S(1)} collective-permute-done((f32[512,64]{0,1:T(8,128)S(1)}, f32[512,64]{0,1:T(8,128)S(1)}, u32[]{:S(2)}, u32[]{:S(2)}) %collective-permute-start.15) | collective-permute-done | bytes 131104 | tf_op jit(solution)/shard_map/ppermute | solution.py:12
  97.0 0.7 bitcast_dynamic-update-slice_fusion
  97.7 2.3 %gather_fusion = f32[12,512,64]{1,2,0:T(8,128)S(1)} fusion(f32[17,512,64]{1,2,0:T(8,128)} %bitcast_dynamic-update-slice_fusion, s32[1024]{0:T(1024)S(1)} %pad_clamp_fusion), kind=kCustom, calls=%fused_computation | custom fusion | bytes 3145776 | tf_op jit(solution)/shard_map/jit(_take)/gather | solution.py:47
  100.1 3.6 %reshape.99 = bf16[128,1,2048]{2,1,0:T(2,128)(2,1)S(1)} reshape(bf16[128,2,1024]{2,1,0:T(2,128)(2,1)} %all-to-all-done) | data formatting | bytes 1048576
  103.7 3.1 %reduce.5 = bf16[128,2048]{1,0:T(8,128)(2,1)S(1)} reduce(bf16[128,1,2048]{2,1,0:T(2,128)(2,1)S(1)} %reshape.99, bf16[]{:T(256)} %constant.43), dimensions={1}, to_apply=%all_to_all.7.reduce_sub_computation | reduce | bytes 1048578 | tf_op jit(solution)/shard_map/all_to_all | solution.py:34
  106.8 1.1 reshape.81
  107.8 3.0 %fusion.26 = f32[64,512]{1,0:T(8,128)S(1)} fusion(bf16[4096,64]{1,0:T(8,128)(2,1)S(1)} %reshape.81, bf16[512,4096]{0,1:T(8,128)(2,1)} %bitcast.53), kind=kOutput, calls=%fused_computation.46 | convolution fusion | flops 268435456 | bytes 4849664 | tf_op jit(solution)/shard_map/dot_general | solution.py:35
  110.9 15.7 %fusion.14 = f32[512,64]{0,1:T(8,128)} fusion(f32[64,512]{1,0:T(8,128)S(1)} %fusion.26, f32[512,6144]{1,0:T(8,128)} %param.8, f32[6144,64]{0,1:T(8,128)S(1)} %bitcast.55, pred[6144]{0:T(1024)(128)(4,1)S(1)} %broadcast_in_dim.50, pred[6144]{0:T(1024)(128)(4,1)S(1)} %broadcast_in_dim.47), kind=kOutput, calls=%fused_computation.9 | convolution fusion | flops 2416738304 | bytes 14430208 | tf_op jit(solution)/shard_map/dot_general | solution.py:49
  (52 shorter events, 11.4 us)
Async XLA Ops:
  0.0 17.2 %copy-start = (s32[128,128]{1,0:T(8,128)S(1)}, s32[128,128]{1,0:T(8,128)}, u32[]{:S(2)}) copy-start(s32[128,128]{1,0:T(8,128)} %param.11) | copy-start | bytes 196612
  0.0 45.7 %collective-permute-start = (f32[512,64]{0,1:T(8,128)}, f32[512,64]{0,1:T(8,128)S(1)}, u32[]{:S(2)}, u32[]{:S(2)}) collective-permute-start(f32[512,64]{0,1:T(8,128)} %param.7), channel_id=1, source_target_pairs={{0,8},{1,9},{2,10},{3,11},{4,12},{5,13},{6,14},{7,15},{8,16},{9,17... | collective-permute-start | bytes 393224 | tf_op jit(solution)/shard_map/ppermute | solution.py:12
  3.3 47.1 %collective-permute-start.1 = (f32[512,64]{0,1:T(8,128)}, f32[512,64]{0,1:T(8,128)S(1)}, u32[]{:S(2)}, u32[]{:S(2)}) collective-permute-start(f32[512,64]{0,1:T(8,128)} %param.7), channel_id=1, source_target_pairs={{0,7},{1,8},{2,9},{3,10},{4,11},{5,12},{6,13},{7,14},{8,15},{9,16}... | collective-permute-start | bytes 393224 | tf_op jit(solution)/shard_map/ppermute | solution.py:12
  7.4 46.2 %collective-permute-start.2 = (f32[512,64]{0,1:T(8,128)}, f32[512,64]{0,1:T(8,128)S(1)}, u32[]{:S(2)}, u32[]{:S(2)}) collective-permute-start(f32[512,64]{0,1:T(8,128)} %param.7), channel_id=1, source_target_pairs={{0,6},{1,7},{2,8},{3,9},{4,10},{5,11},{6,12},{7,13},{8,14},{9,15},... | collective-permute-start | bytes 393224 | tf_op jit(solution)/shard_map/ppermute | solution.py:12
  10.6 46.8 %collective-permute-start.3 = (f32[512,64]{0,1:T(8,128)}, f32[512,64]{0,1:T(8,128)S(1)}, u32[]{:S(2)}, u32[]{:S(2)}) collective-permute-start(f32[512,64]{0,1:T(8,128)} %param.7), channel_id=1, source_target_pairs={{0,5},{1,6},{2,7},{3,8},{4,9},{5,10},{6,11},{7,12},{8,13},{9,14},{... | collective-permute-start | bytes 393224 | tf_op jit(solution)/shard_map/ppermute | solution.py:12
  15.0 45.0 %collective-permute-start.4 = (f32[512,64]{0,1:T(8,128)}, f32[512,64]{0,1:T(8,128)S(1)}, u32[]{:S(2)}, u32[]{:S(2)}) collective-permute-start(f32[512,64]{0,1:T(8,128)} %param.7), channel_id=1, source_target_pairs={{0,4},{1,5},{2,6},{3,7},{4,8},{5,9},{6,10},{7,11},{8,12},{9,13},{1... | collective-permute-start | bytes 393224 | tf_op jit(solution)/shard_map/ppermute | solution.py:12
  21.2 14.3 %copy-start.2 = (s32[128,12]{0,1:T(8,128)S(1)}, s32[128,12]{0,1:T(8,128)}, u32[]{:S(2)}) copy-start(s32[128,12]{0,1:T(8,128)} %param.12) | copy-start | bytes 18436
  21.2 14.5 %copy-start.3 = (s32[128]{0:T(128)S(1)}, s32[128]{0:T(128)}, u32[]{:S(2)}) copy-start(s32[128]{0:T(128)} %param.13) | copy-start | bytes 1540
  24.1 76.0 %all-to-all-start = ((bf16[128,2,1024]{2,1,0:T(2,128)(2,1)}), bf16[128,2,1024]{2,1,0:T(2,128)(2,1)}, u32[]{:S(2)}, u32[]{:S(2)}) async-start(bf16[128,2,1024]{2,1,0:T(2,128)(2,1)} %reshape.98), calls=%async_computation | async-start | bytes 1048576 | tf_op jit(solution)/shard_map/all_to_all | solution.py:34
  36.9 8.8 %copy-start.1 = (f32[512,64]{0,1:T(8,128)S(1)}, f32[512,64]{0,1:T(8,128)}, u32[]{:S(2)}) copy-start(f32[512,64]{0,1:T(8,128)} %param.7) | copy-start | bytes 393220
  45.8 17.0 %collective-permute-start.5 = (f32[512,64]{0,1:T(8,128)S(1)}, f32[512,64]{0,1:T(8,128)S(1)}, u32[]{:S(2)}, u32[]{:S(2)}) collective-permute-start(f32[512,64]{0,1:T(8,128)S(1)} %copy-done.1), channel_id=1, source_target_pairs={{0,3},{1,4},{2,5},{3,6},{4,7},{5,8},{6,9},{7,10},{8,11},{9,12},{10... | collective-permute-start | bytes 393224 | tf_op jit(solution)/shard_map/ppermute | solution.py:12
  50.4 18.5 %collective-permute-start.6 = (f32[512,64]{0,1:T(8,128)S(1)}, f32[512,64]{0,1:T(8,128)S(1)}, u32[]{:S(2)}, u32[]{:S(2)}) collective-permute-start(f32[512,64]{0,1:T(8,128)S(1)} %copy-done.1), channel_id=1, source_target_pairs={{0,2},{1,3},{2,4},{3,5},{4,6},{5,7},{6,8},{7,9},{8,10},{9,11},{10,... | collective-permute-start | bytes 393224 | tf_op jit(solution)/shard_map/ppermute | solution.py:12
  53.6 17.9 %collective-permute-start.7 = (f32[512,64]{0,1:T(8,128)S(1)}, f32[512,64]{0,1:T(8,128)S(1)}, u32[]{:S(2)}, u32[]{:S(2)}) collective-permute-start(f32[512,64]{0,1:T(8,128)S(1)} %copy-done.1), channel_id=1, source_target_pairs={{0,1},{1,2},{2,3},{3,4},{4,5},{5,6},{6,7},{7,8},{8,9},{9,10},{10,1... | collective-permute-start | bytes 393224 | tf_op jit(solution)/shard_map/ppermute | solution.py:12
  57.4 20.6 %collective-permute-start.8 = (f32[512,64]{0,1:T(8,128)S(1)}, f32[512,64]{0,1:T(8,128)S(1)}, u32[]{:S(2)}, u32[]{:S(2)}) collective-permute-start(f32[512,64]{0,1:T(8,128)S(1)} %copy-done.1), channel_id=1, source_target_pairs={{1,0},{2,1},{3,2},{4,3},{5,4},{6,5},{7,6},{8,7},{9,8},{10,9},{11,1... | collective-permute-start | bytes 393224 | tf_op jit(solution)/shard_map/ppermute | solution.py:12
  60.0 21.9 %collective-permute-start.9 = (f32[512,64]{0,1:T(8,128)S(1)}, f32[512,64]{0,1:T(8,128)S(1)}, u32[]{:S(2)}, u32[]{:S(2)}) collective-permute-start(f32[512,64]{0,1:T(8,128)S(1)} %copy-done.1), channel_id=1, source_target_pairs={{2,0},{3,1},{4,2},{5,3},{6,4},{7,5},{8,6},{9,7},{10,8},{11,9},{12,... | collective-permute-start | bytes 393224 | tf_op jit(solution)/shard_map/ppermute | solution.py:12
  62.8 24.9 %collective-permute-start.10 = (f32[512,64]{0,1:T(8,128)S(1)}, f32[512,64]{0,1:T(8,128)S(1)}, u32[]{:S(2)}, u32[]{:S(2)}) collective-permute-start(f32[512,64]{0,1:T(8,128)S(1)} %copy-done.1), channel_id=1, source_target_pairs={{3,0},{4,1},{5,2},{6,3},{7,4},{8,5},{9,6},{10,7},{11,8},{12,9},{13... | collective-permute-start | bytes 393224 | tf_op jit(solution)/shard_map/ppermute | solution.py:12
  68.9 21.8 %collective-permute-start.11 = (f32[512,64]{0,1:T(8,128)S(1)}, f32[512,64]{0,1:T(8,128)S(1)}, u32[]{:S(2)}, u32[]{:S(2)}) collective-permute-start(f32[512,64]{0,1:T(8,128)S(1)} %copy-done.1), channel_id=1, source_target_pairs={{4,0},{5,1},{6,2},{7,3},{8,4},{9,5},{10,6},{11,7},{12,8},{13,9},{1... | collective-permute-start | bytes 393224 | tf_op jit(solution)/shard_map/ppermute | solution.py:12
  71.4 19.9 %collective-permute-start.12 = (f32[512,64]{0,1:T(8,128)S(1)}, f32[512,64]{0,1:T(8,128)S(1)}, u32[]{:S(2)}, u32[]{:S(2)}) collective-permute-start(f32[512,64]{0,1:T(8,128)S(1)} %copy-done.1), channel_id=1, source_target_pairs={{5,0},{6,1},{7,2},{8,3},{9,4},{10,5},{11,6},{12,7},{13,8},{14,9},{... | collective-permute-start | bytes 393224 | tf_op jit(solution)/shard_map/ppermute | solution.py:12
  77.9 14.1 %collective-permute-start.13 = (f32[512,64]{0,1:T(8,128)S(1)}, f32[512,64]{0,1:T(8,128)S(1)}, u32[]{:S(2)}, u32[]{:S(2)}) collective-permute-start(f32[512,64]{0,1:T(8,128)S(1)} %copy-done.1), channel_id=1, source_target_pairs={{6,0},{7,1},{8,2},{9,3},{10,4},{11,5},{12,6},{13,7},{14,8},{15,9},... | collective-permute-start | bytes 393224 | tf_op jit(solution)/shard_map/ppermute | solution.py:12
  81.8 10.8 %collective-permute-start.14 = (f32[512,64]{0,1:T(8,128)S(1)}, f32[512,64]{0,1:T(8,128)S(1)}, u32[]{:S(2)}, u32[]{:S(2)}) collective-permute-start(f32[512,64]{0,1:T(8,128)S(1)} %copy-done.1), channel_id=1, source_target_pairs={{7,0},{8,1},{9,2},{10,3},{11,4},{12,5},{13,6},{14,7},{15,8},{16,9}... | collective-permute-start | bytes 393224 | tf_op jit(solution)/shard_map/ppermute | solution.py:12
  87.7 9.3 %collective-permute-start.15 = (f32[512,64]{0,1:T(8,128)S(1)}, f32[512,64]{0,1:T(8,128)S(1)}, u32[]{:S(2)}, u32[]{:S(2)}) collective-permute-start(f32[512,64]{0,1:T(8,128)S(1)} %copy-done.1), channel_id=1, source_target_pairs={{8,0},{9,1},{10,2},{11,3},{12,4},{13,5},{14,6},{15,7},{16,8},{17,9... | collective-permute-start | bytes 393224 | tf_op jit(solution)/shard_map/ppermute | solution.py:12
where the time goes:
time: 128 us; the launch traced here: 127 us
  starting transfers between devices  65.2 us (51%)
  local copies, waits for them, and re-layouts  29.9 us (23%)
  matrix products  22.5 us (18%)
  other arithmetic  4.95 us (4%)
  waiting for transfers between devices  3.72 us (3%)
    ppermute x16, starting transfers between devices, shifted(): lax.ppermute(value, axis, [(source, source + steps) for source in range(i...  53.9 us
    unnamed x28, local copies, waits for them, and re-layouts  24.2 us
    dot_general x1, matrix products, body(): jnp.dot(near_blocks, gathered.reshape(slot_total * strip_rows, sides), pr...  15.7 us
    all_to_all x1, starting transfers between devices, body(): lax.all_to_all(outgoing, 'strip', split_axis=0, concat_axis=0, tiled=True)  11.3 us
    all_to_all x2, other arithmetic, body(): lax.all_to_all(outgoing, 'strip', split_axis=0, concat_axis=0, tiled=True)  4.08 us
    dot_general x1, matrix products, body(): jnp.einsum('mik,mr->ikr', v_far, source_bf, preferred_element_type=jnp.fl...  3.73 us
    ppermute x16, waiting for transfers between devices, shifted(): lax.ppermute(value, axis, [(source, source + steps) for source in range(i...  3.72 us
    dot_general x1, matrix products, body(): jnp.dot(u_far.reshape(strip_rows, strips * rank_max), incoming.reshape(st...  3.04 us
  transfers between devices with their start and end apart: 17, of which 1 were waited for; matrix products, arithmetic and copies ran while one was open for 24% of the time, Pallas kernels for 0%

commit v1 on v0

v1 whole, which is shorter than its diff:
```python
import functools

import jax
import jax.numpy as jnp
from jax import lax
from jax.experimental import pallas as pl
from jax.experimental.pallas import tpu as pltpu
from jax.sharding import PartitionSpec as P

WINDOW = 8
REACH = WINDOW // 2

bf16 = jnp.bfloat16
f32 = jnp.float32
MiB = 2**20


def project_kernel(chunk, me_ref, x_ref, ranks_ref, v_ref, out_ref, raw_ref, turned_ref, sems):
    rows, rank_max, strips = raw_ref.shape
    parts = rows // chunk
    copies = [
        pltpu.make_async_copy(
            v_ref.at[pl.ds(n * chunk, chunk)], raw_ref.at[pl.ds(n * chunk, chunk)], sems.at[n]
        )
        for n in range(parts)
    ]
    for copy in copies:
        copy.start()
    source = x_ref[...].astype(bf16)
    hot = (lax.broadcasted_iota(jnp.int32, (8, strips), 1) == me_ref[0]).astype(bf16)
    rank = lax.dot_general(
        hot,
        ranks_ref[...].astype(f32).astype(bf16),
        (((1,), (1,)), ((), ())),
        preferred_element_type=f32,
    )
    rank = jnp.broadcast_to(rank[:1], (source.shape[0], strips))
    for n in range(parts):
        copies[n].wait()
        turned_ref[:, pl.ds(n * chunk, chunk), :] = jnp.swapaxes(
            raw_ref[pl.ds(n * chunk, chunk)], 0, 1
        )
    factors = jnp.concatenate([turned_ref[k] for k in range(rank_max)], axis=1)
    product = jnp.dot(source, factors, preferred_element_type=f32)
    kept = [
        jnp.where(rank > k, product[:, k * strips : (k + 1) * strips], 0.0).astype(bf16)
        for k in range(rank_max)
    ]
    pairs = [jnp.concatenate(kept[k : k + 2], axis=0).T for k in range(0, rank_max, 2)]
    out_ref[...] = jnp.swapaxes(jnp.stack(pairs), 0, 1)


def project(me, source, ranks, v_turned):
    rows, rank_max, strips = v_turned.shape
    sides = source.shape[0]
    chunk = 64
    return pl.pallas_call(
        functools.partial(project_kernel, chunk),
        in_specs=[
            pl.BlockSpec(memory_space=pltpu.SMEM),
            pl.BlockSpec(memory_space=pltpu.VMEM),
            pl.BlockSpec(memory_space=pltpu.VMEM),
            pl.BlockSpec(memory_space=pl.ANY),
        ],
        out_specs=pl.BlockSpec(memory_space=pltpu.VMEM),
        out_shape=jax.ShapeDtypeStruct((strips, rank_max // 2, 2 * sides), bf16),
        scratch_shapes=[
            pltpu.VMEM((rows, rank_max, strips), bf16),
            pltpu.VMEM((rank_max, rows, strips), bf16),
            pltpu.SemaphoreType.DMA((rows // chunk,)),
        ],
        compiler_params=pltpu.CompilerParams(vmem_limit_bytes=28 * MiB),
        cost_estimate=pl.CostEstimate(
            flops=2 * rows * rank_max * strips * sides,
            bytes_accessed=2 * rows * rank_max * strips,
            transcendentals=0,
        ),
        name="project",
    )(me, source, ranks, v_turned)


def near_kernel(me_ref, list_ref, count_ref, blocks_ref, pair_ref, *refs):
    direct, swapped, (out_ref, table_ref, tiles_ref, sems) = (
        refs[:REACH],
        refs[REACH : 2 * REACH],
        refs[2 * REACH :],
    )
    slots = list_ref.shape[0]
    rows = tiles_ref.shape[1]
    me = me_ref[0]
    core = me % 2
    copies = [
        pltpu.make_async_copy(
            blocks_ref.at[:, pl.ds(s * rows, rows)], tiles_ref.at[s], sems.at[s]
        )
        for s in range(slots)
    ]
    for copy in copies:
        copy.start()
    for n, ref in enumerate((pair_ref, *direct, *swapped)):
        table_ref[pl.ds(2 * n, 2)] = ref[...]
    total = jnp.zeros(out_ref.shape, f32)
    for s in range(slots):
        strip = list_ref[s, me]
        live = s < count_ref[me]
        chips = strip // 2 - me // 2
        distance = jnp.abs(chips)
        is_own = distance == 0
        is_direct = (chips > 0) == (core == 0)
        sender_core = jnp.where(jnp.logical_or(is_own, is_direct), core, 1 - core)
        group = jnp.where(is_own, 0, distance + jnp.where(is_direct, 0, REACH))
        place = jnp.clip(2 * group + jnp.where(strip % 2 == sender_core, 0, 1), 0, table_ref.shape[0] - 1)
        strip_density = table_ref[place]
        strip_density = jnp.where(live, strip_density, jnp.zeros_like(strip_density))
        copies[s].wait()
        tile = tiles_ref[s]
        high = tile.astype(bf16)
        low = (tile - high.astype(f32)).astype(bf16)
        for piece in (high, low):
            total += lax.dot_general(
                strip_density, piece, (((1,), (1,)), ((), ())), preferred_element_type=f32
            )
    out_ref[...] = total


def near(me, near_list, near_count, near_blocks, pair, direct, swapped):
    rows = near_blocks.shape[0]
    slots = near_list.shape[1]
    sides = pair.shape[1]
    smem = pl.BlockSpec(memory_space=pltpu.SMEM)
    vmem = pl.BlockSpec(memory_space=pltpu.VMEM)
    return pl.pallas_call(
        near_kernel,
        in_specs=[smem, smem, smem, pl.BlockSpec(memory_space=pl.ANY)] + [vmem] * (1 + 2 * REACH),
        out_specs=vmem,
        out_shape=jax.ShapeDtypeStruct((sides, rows), f32),
        scratch_shapes=[
            pltpu.VMEM((2 + 4 * REACH, sides, rows), bf16),
            pltpu.VMEM((slots, rows, rows), f32),
            pltpu.SemaphoreType.DMA((slots,)),
        ],
        compiler_params=pltpu.CompilerParams(vmem_limit_bytes=32 * MiB),
        cost_estimate=pl.CostEstimate(
            flops=4 * rows * rows * slots * sides,
            bytes_accessed=4 * rows * rows * slots,
            transcendentals=0,
        ),
        name="near",
    )(me, near_list.T, near_count, near_blocks, pair, *direct, *swapped)


def far_kernel(chunk, near_ref, u_ref, coefficients_ref, out_ref, raw_ref, turned_ref, sems):
    rows, rank_max, strips = raw_ref.shape
    sides = out_ref.shape[0]
    parts = rows // chunk
    copies = [
        pltpu.make_async_copy(
            u_ref.at[pl.ds(n * chunk, chunk)], raw_ref.at[pl.ds(n * chunk, chunk)], sems.at[n]
        )
        for n in range(parts)
    ]
    for copy in copies:
        copy.start()
    turned = jnp.swapaxes(coefficients_ref[...], 0, 1)
    weights = jnp.concatenate(
        [
            turned[p][:, half * sides : (half + 1) * sides]
            for p in range(rank_max // 2)
            for half in range(2)
        ],
        axis=0,
    )
    for n in range(parts):
        copies[n].wait()
        turned_ref[:, pl.ds(n * chunk, chunk), :] = jnp.swapaxes(
            raw_ref[pl.ds(n * chunk, chunk)], 0, 1
        )
    factors = jnp.concatenate([turned_ref[k] for k in range(rank_max)], axis=1)
    far = jnp.dot(factors, weights, preferred_element_type=f32)
    out_ref[...] = near_ref[...] + far.T


def add_far(near_field, u_turned, coefficients):
    rows, rank_max, strips = u_turned.shape
    sides = near_field.shape[0]
    chunk = 64
    vmem = pl.BlockSpec(memory_space=pltpu.VMEM)
    return pl.pallas_call(
        functools.partial(far_kernel, chunk),
        in_specs=[vmem, pl.BlockSpec(memory_space=pl.ANY), vmem],
        out_specs=vmem,
        out_shape=jax.ShapeDtypeStruct((sides, rows), f32),
        scratch_shapes=[
            pltpu.VMEM((rows, rank_max, strips), bf16),
            pltpu.VMEM((rank_max, rows, strips), bf16),
            pltpu.SemaphoreType.DMA((rows // chunk,)),
        ],
        compiler_params=pltpu.CompilerParams(vmem_limit_bytes=28 * MiB),
        cost_estimate=pl.CostEstimate(
            flops=2 * rows * rank_max * strips * sides,
            bytes_accessed=2 * rows * rank_max * strips,
            transcendentals=0,
        ),
        name="add_far",
    )(near_field, u_turned, coefficients)


def body(density, near_blocks, u_far, v_far, ranks, near_list, near_count):
    strips = lax.axis_size("strip")
    pairs = strips // 2
    me = lax.axis_index("strip").astype(jnp.int32).reshape(1)
    source = density.T
    swap = [(d, d ^ 1) for d in range(strips)]
    sibling = lax.ppermute(source, "strip", swap)
    outgoing = project(me, source, ranks, jnp.transpose(v_far, (0, 2, 1)))
    source, sibling, outgoing = lax.optimization_barrier((source, sibling, outgoing))
    incoming = lax.all_to_all(outgoing, "strip", split_axis=0, concat_axis=0, tiled=True)
    pair = jnp.stack([source.astype(bf16), sibling.astype(bf16)])
    direct = []
    swapped = []
    for step in range(1, REACH + 1):
        moves = [(2 * (c + step), 2 * c) for c in range(pairs - step)]
        moves += [(2 * c + 1, 2 * (c + step) + 1) for c in range(pairs - step)]
        direct.append(lax.ppermute(pair, "strip", moves))
    for block in direct:
        swapped.append(lax.ppermute(block, "strip", swap))
    near_field = near(me, near_list, near_count, near_blocks, pair, direct, swapped)
    return add_far(near_field, jnp.transpose(u_far, (0, 2, 1)), incoming).T


def solution(mesh):
    return jax.shard_map(
        body,
        mesh=mesh,
        in_specs=(
            P("strip", None),
            P("strip", None),
            P("strip", None, None),
            P("strip", None, None),
            P(),
            P(),
            P(),
        ),
        out_specs=P("strip", None),
        check_vma=False,
    )
```

time: 128 us -> 59.7 us (0.47)
  the two profiles are of different devices: /device:TPU:59 before, /device:TPU:33 now
where the time goes in v1:
time: 59.7 us; the launch traced here: 59.3 us
  starting transfers between devices  27.8 us (47%)
  Pallas kernels  14.5 us (24%)
  local copies, waits for them, and re-layouts  10.7 us (18%)
  waiting for transfers between devices  5.11 us (9%)
  other arithmetic  1.01 us (2%)
    ppermute x4, starting transfers between devices, body(): direct.append(lax.ppermute(pair, 'strip', moves))  13.4 us
    unnamed x16, local copies, waits for them, and re-layouts  10.7 us
    all_to_all x1, starting transfers between devices, body(): lax.all_to_all(outgoing, 'strip', split_axis=0, concat_axis=0, tiled=True)  9.98 us
    pallas_call x1, Pallas kernels, near(): pl.pallas_call(near_kernel, in_specs=[smem, smem, smem, pl.BlockSpec(memo...  7.3 us
    ppermute x4, waiting for transfers between devices, body(): direct.append(lax.ppermute(pair, 'strip', moves))  3.77 us
    pallas_call x1, Pallas kernels, add_far(): pl.pallas_call(functools.partial(far_kernel, chunk), in_specs=[vmem, pl.B...  3.69 us
    ppermute x4, starting transfers between devices, body(): swapped.append(lax.ppermute(block, 'strip', swap))  3.64 us
    pallas_call x1, Pallas kernels, project(): pl.pallas_call(functools.partial(project_kernel, chunk), in_specs=[pl.Blo...  3.54 us
  transfers between devices with their start and end apart: 10, of which 3 were waited for; matrix products, arithmetic and copies ran while one was open for 0% of the time, Pallas kernels for 18%

profile of v1, /device:TPU:33, one launch (start us, length us, event | category | flops | bytes accessed | tf_op | source)
XLA Modules:
  0.0 59.3 jit_solution(11034621501416949038)
XLA Ops:
  0.0 1.0 %bitcast_convert_fusion = bf16[64,512]{1,0:T(8,128)(2,1)S(1)} fusion(f32[512,64]{0,1:T(8,128)} %param.7), kind=kLoop, calls=%fused_computation.3 | loop fusion | flops 32768 | bytes 196608
  1.0 0.8 %collective-permute-start = (bf16[64,512]{1,0:T(8,128)(2,1)S(1)}, bf16[64,512]{1,0:T(8,128)(2,1)S(1)}, u32[]{:S(2)}, u32[]{:S(2)}) collective-permute-start(bf16[64,512]{1,0:T(8,128)(2,1)S(1)} %bitcast_convert_fusion), channel_id=1, source_target_pairs={{0,1},{1,0},{2,3},{3,2},{4,5},{5,4},{6,7},{7,6},{8,9},{9,8},{10,11... | collective-permute-start | bytes 196616 | tf_op jit(solution)/shard_map/ppermute | solution.py:214
  1.7 2.2 %copy-done.1 = bf16[512,128,32]{1,2,0:T(8,128)(2,1)S(1)} copy-done((bf16[512,128,32]{1,2,0:T(8,128)(2,1)S(1)}, bf16[512,128,32]{1,2,0:T(8,128)(2,1)}, u32[]{:S(2)}) %copy-start.1) | copy-done | bytes 4194328
  3.9 0.9 %copy-done.3 = f32[512,64]{0,1:T(8,128)S(1)} copy-done((f32[512,64]{0,1:T(8,128)S(1)}, f32[512,64]{0,1:T(8,128)}, u32[]{:S(2)}) %copy-start.3) | copy-done | bytes 131096
  4.8 0.8 %copy-done.5 = s32[128,128]{1,0:T(8,128)S(1)} copy-done((s32[128,128]{1,0:T(8,128)S(1)}, s32[128,128]{1,0:T(8,128)}, u32[]{:S(2)}) %copy-start.5) | copy-done | bytes 65560
  5.7 3.5 %project.1 = bf16[128,16,128]{2,1,0:T(8,128)(2,1)} custom-call(s32[1]{0:T(128)} %bitcast.me_ref, f32[64,512]{1,0:T(8,128)S(1)} %bitcast.14, s32[128,128]{1,0:T(8,128)S(1)} %copy-done.5, bf16[512,32,128]{2,1,0:T(8,128)(2,1)S(1)} %bitcast.12), custom_call_target="tpu_custom_call" | custom-call | flops 268435456 | bytes 4194304 | tf_op jit(solution)/shard_map/project/pallas_call | solution.py:57
  9.2 0.0 collective-permute-done
  9.2 10.0 %all-to-all-start = ((bf16[128,16,128]{2,1,0:T(8,128)(2,1)}), bf16[128,16,128]{2,1,0:T(8,128)(2,1)S(1)}, u32[]{:S(2)}, u32[]{:S(2)}) async-start(bf16[128,16,128]{2,1,0:T(8,128)(2,1)} %project.1), calls=%async_computation | async-start | bytes 1048576 | tf_op jit(solution)/shard_map/all_to_all | solution.py:217
  19.2 0.0 copy-done.4
  19.3 3.2 %collective-permute-start.4 = (bf16[2,64,512]{2,1,0:T(8,128)(2,1)S(1)}, bf16[2,64,512]{2,1,0:T(8,128)(2,1)S(1)}, u32[]{:S(2)}, u32[]{:S(2)}) collective-permute-start(bf16[2,64,512]{2,1,0:T(8,128)(2,1)S(1)} %pad_maximum_fusion.pair_ref), channel_id=1, source_target_pairs={{8,0},{10,2},{12,4},{14,6},{16,8},{18,10},{20,12},{22,14},{24,16},... | collective-permute-start | bytes 393224 | tf_op jit(solution)/shard_map/ppermute | solution.py:224
  22.4 4.4 %collective-permute-start.3 = (bf16[2,64,512]{2,1,0:T(8,128)(2,1)S(1)}, bf16[2,64,512]{2,1,0:T(8,128)(2,1)S(1)}, u32[]{:S(2)}, u32[]{:S(2)}) collective-permute-start(bf16[2,64,512]{2,1,0:T(8,128)(2,1)S(1)} %pad_maximum_fusion.pair_ref), channel_id=1, source_target_pairs={{6,0},{8,2},{10,4},{12,6},{14,8},{16,10},{18,12},{20,14},{22,16},{... | collective-permute-start | bytes 393224 | tf_op jit(solution)/shard_map/ppermute | solution.py:224
  26.8 3.4 %collective-permute-start.2 = (bf16[2,64,512]{2,1,0:T(8,128)(2,1)S(1)}, bf16[2,64,512]{2,1,0:T(8,128)(2,1)S(1)}, u32[]{:S(2)}, u32[]{:S(2)}) collective-permute-start(bf16[2,64,512]{2,1,0:T(8,128)(2,1)S(1)} %pad_maximum_fusion.pair_ref), channel_id=1, source_target_pairs={{4,0},{6,2},{8,4},{10,6},{12,8},{14,10},{16,12},{18,14},{20,16},{2... | collective-permute-start | bytes 393224 | tf_op jit(solution)/shard_map/ppermute | solution.py:224
  30.2 2.5 %collective-permute-start.1 = (bf16[2,64,512]{2,1,0:T(8,128)(2,1)S(1)}, bf16[2,64,512]{2,1,0:T(8,128)(2,1)S(1)}, u32[]{:S(2)}, u32[]{:S(2)}) collective-permute-start(bf16[2,64,512]{2,1,0:T(8,128)(2,1)S(1)} %pad_maximum_fusion.pair_ref), channel_id=1, source_target_pairs={{2,0},{4,2},{6,4},{8,6},{10,8},{12,10},{14,12},{16,14},{18,16},{20... | collective-permute-start | bytes 393224 | tf_op jit(solution)/shard_map/ppermute | solution.py:224
  32.7 0.0 collective-permute-done.4.refs_3_
  32.7 3.1 %collective-permute-start.8 = (bf16[2,64,512]{2,1,0:T(8,128)(2,1)S(1)}, bf16[2,64,512]{2,1,0:T(8,128)(2,1)S(1)}, u32[]{:S(2)}, u32[]{:S(2)}) collective-permute-start(bf16[2,64,512]{2,1,0:T(8,128)(2,1)S(1)} %collective-permute-done.4.refs_3_), channel_id=1, source_target_pairs={{0,1},{1,0},{2,3},{3,2},{4,5},{5,4},{6,7},{7,6},{8,9},{9,8},{10,11... | collective-permute-start | bytes 393224 | tf_op jit(solution)/shard_map/ppermute | solution.py:226
  35.8 0.0 collective-permute-done.3.refs_2_
  35.8 0.1 collective-permute-start.7
  35.9 1.1 %collective-permute-done.2.refs_1_ = bf16[2,64,512]{2,1,0:T(8,128)(2,1)S(1)} collective-permute-done((bf16[2,64,512]{2,1,0:T(8,128)(2,1)S(1)}, bf16[2,64,512]{2,1,0:T(8,128)(2,1)S(1)}, u32[]{:S(2)}, u32[]{:S(2)}) %collective-permute-start.2) | collective-permute-done | bytes 131104 | tf_op jit(solution)/shard_map/ppermute | solution.py:224
  37.0 0.4 collective-permute-start.6
  37.5 2.7 %collective-permute-done.1.refs_0_ = bf16[2,64,512]{2,1,0:T(8,128)(2,1)S(1)} collective-permute-done((bf16[2,64,512]{2,1,0:T(8,128)(2,1)S(1)}, bf16[2,64,512]{2,1,0:T(8,128)(2,1)S(1)}, u32[]{:S(2)}, u32[]{:S(2)}) %collective-permute-start.1) | collective-permute-done | bytes 131104 | tf_op jit(solution)/shard_map/ppermute | solution.py:224
  40.2 0.0 collective-permute-start.5
  40.2 0.0 collective-permute-done.8.refs_7_
  40.2 0.0 collective-permute-done.7.refs_6_
  40.2 0.0 collective-permute-done.6.refs_5_
  40.2 1.3 %collective-permute-done.5.refs_4_ = bf16[2,64,512]{2,1,0:T(8,128)(2,1)S(1)} collective-permute-done((bf16[2,64,512]{2,1,0:T(8,128)(2,1)S(1)}, bf16[2,64,512]{2,1,0:T(8,128)(2,1)S(1)}, u32[]{:S(2)}, u32[]{:S(2)}) %collective-permute-start.5) | collective-permute-done | bytes 131104 | tf_op jit(solution)/shard_map/ppermute | solution.py:226
  41.5 0.0 copy-done.7
  41.5 4.6 %copy-done = f32[512,6144]{1,0:T(8,128)S(1)} copy-done((f32[512,6144]{1,0:T(8,128)S(1)}, f32[512,6144]{1,0:T(8,128)}, u32[]{:S(2)}) %copy-start) | copy-done | bytes 12582936
  46.1 7.3 %near.1.near_ref = f32[64,512]{1,0:T(8,128)S(1)} custom-call(s32[1]{0:T(128)} %bitcast.me_ref, s32[12,128]{1,0:T(8,128)S(1)} %bitcast.16, s32[128]{0:T(128)S(1)} %copy-done.7, f32[512,6144]{1,0:T(8,128)S(1)} %copy-done, bf16[2,64,512]{2,1,0:T(8,128)(2,1)S(1)} %pad_maximum_fusion.pair_ref, bf16[2,64,512]{2,1,0:T(8,128)(2,1)S(1)} %collective-permute-done.1.refs_0_, ...), custom_call_target="tpu_custom_call" | custom-call | flops 805306368 | bytes 12582912 | tf_op jit(solution)/shard_map/near/pallas_call | solution.py:132
  53.4 0.0 all-to-all-done.coefficients_ref
  53.4 0.0 copy-start.2
  53.4 2.2 %copy-done.2 = bf16[512,128,32]{1,2,0:T(8,128)(2,1)S(1)} copy-done((bf16[512,128,32]{1,2,0:T(8,128)(2,1)S(1)}, bf16[512,128,32]{1,2,0:T(8,128)(2,1)}, u32[]{:S(2)}) %copy-start.2) | copy-done | bytes 4194328
  55.6 3.7 %add_far.1 = f32[64,512]{1,0:T(8,128)} custom-call(f32[64,512]{1,0:T(8,128)S(1)} %near.1.near_ref, bf16[512,32,128]{2,1,0:T(8,128)(2,1)S(1)} %bitcast.13, bf16[128,16,128]{2,1,0:T(8,128)(2,1)S(1)} %all-to-all-done.coefficients_ref), custom_call_target="tpu_custom_call" | custom-call | flops 268435456 | bytes 4194304 | tf_op jit(solution)/shard_map/add_far/pallas_call | solution.py:188
  (10 shorter events, 0.0 us)
Async XLA Ops:
  0.0 19.2 %copy-start.4 = (f32[512,64]{0,1:T(8,128)S(1)}, f32[512,64]{0,1:T(8,128)}, u32[]{:S(2)}) copy-start(f32[512,64]{0,1:T(8,128)} %param.7) | copy-start | bytes 393220
  0.0 41.5 %copy-start.7 = (s32[128]{0:T(128)S(1)}, s32[128]{0:T(128)}, u32[]{:S(2)}) copy-start(s32[128]{0:T(128)} %count_ref.1) | copy-start | bytes 1540
  0.0 41.5 %copy-start.6 = (s32[128,12]{0,1:T(8,128)S(1)}, s32[128,12]{0,1:T(8,128)}, u32[]{:S(2)}) copy-start(s32[128,12]{0,1:T(8,128)} %param.12) | copy-start | bytes 18436
  1.0 8.2 %collective-permute-start = (bf16[64,512]{1,0:T(8,128)(2,1)S(1)}, bf16[64,512]{1,0:T(8,128)(2,1)S(1)}, u32[]{:S(2)}, u32[]{:S(2)}) collective-permute-start(bf16[64,512]{1,0:T(8,128)(2,1)S(1)} %bitcast_convert_fusion), channel_id=1, source_target_pairs={{0,1},{1,0},{2,3},{3,2},{4,5},{5,4},{6,7},{7,6},{8,9},{9,8},{10,11... | collective-permute-start | bytes 196616 | tf_op jit(solution)/shard_map/ppermute | solution.py:214
  1.7 2.2 %copy-start.1 = (bf16[512,128,32]{1,2,0:T(8,128)(2,1)S(1)}, bf16[512,128,32]{1,2,0:T(8,128)(2,1)}, u32[]{:S(2)}) copy-start(bf16[512,128,32]{1,2,0:T(8,128)(2,1)} %param.10) | copy-start | bytes 12582916
  3.9 0.9 %copy-start.3 = (f32[512,64]{0,1:T(8,128)S(1)}, f32[512,64]{0,1:T(8,128)}, u32[]{:S(2)}) copy-start(f32[512,64]{0,1:T(8,128)} %param.7) | copy-start | bytes 393220
  4.8 0.8 %copy-start.5 = (s32[128,128]{1,0:T(8,128)S(1)}, s32[128,128]{1,0:T(8,128)}, u32[]{:S(2)}) copy-start(s32[128,128]{1,0:T(8,128)} %ranks_ref.1) | copy-start | bytes 196612
  9.2 44.2 %all-to-all-start = ((bf16[128,16,128]{2,1,0:T(8,128)(2,1)}), bf16[128,16,128]{2,1,0:T(8,128)(2,1)S(1)}, u32[]{:S(2)}, u32[]{:S(2)}) async-start(bf16[128,16,128]{2,1,0:T(8,128)(2,1)} %project.1), calls=%async_computation | async-start | bytes 1048576 | tf_op jit(solution)/shard_map/all_to_all | solution.py:217
  19.3 13.5 %collective-permute-start.4 = (bf16[2,64,512]{2,1,0:T(8,128)(2,1)S(1)}, bf16[2,64,512]{2,1,0:T(8,128)(2,1)S(1)}, u32[]{:S(2)}, u32[]{:S(2)}) collective-permute-start(bf16[2,64,512]{2,1,0:T(8,128)(2,1)S(1)} %pad_maximum_fusion.pair_ref), channel_id=1, source_target_pairs={{8,0},{10,2},{12,4},{14,6},{16,8},{18,10},{20,12},{22,14},{24,16},... | collective-permute-start | bytes 393224 | tf_op jit(solution)/shard_map/ppermute | solution.py:224
  22.4 13.4 %collective-permute-start.3 = (bf16[2,64,512]{2,1,0:T(8,128)(2,1)S(1)}, bf16[2,64,512]{2,1,0:T(8,128)(2,1)S(1)}, u32[]{:S(2)}, u32[]{:S(2)}) collective-permute-start(bf16[2,64,512]{2,1,0:T(8,128)(2,1)S(1)} %pad_maximum_fusion.pair_ref), channel_id=1, source_target_pairs={{6,0},{8,2},{10,4},{12,6},{14,8},{16,10},{18,12},{20,14},{22,16},{... | collective-permute-start | bytes 393224 | tf_op jit(solution)/shard_map/ppermute | solution.py:224
  26.8 10.2 %collective-permute-start.2 = (bf16[2,64,512]{2,1,0:T(8,128)(2,1)S(1)}, bf16[2,64,512]{2,1,0:T(8,128)(2,1)S(1)}, u32[]{:S(2)}, u32[]{:S(2)}) collective-permute-start(bf16[2,64,512]{2,1,0:T(8,128)(2,1)S(1)} %pad_maximum_fusion.pair_ref), channel_id=1, source_target_pairs={{4,0},{6,2},{8,4},{10,6},{12,8},{14,10},{16,12},{18,14},{20,16},{2... | collective-permute-start | bytes 393224 | tf_op jit(solution)/shard_map/ppermute | solution.py:224
  30.2 9.9 %collective-permute-start.1 = (bf16[2,64,512]{2,1,0:T(8,128)(2,1)S(1)}, bf16[2,64,512]{2,1,0:T(8,128)(2,1)S(1)}, u32[]{:S(2)}, u32[]{:S(2)}) collective-permute-start(bf16[2,64,512]{2,1,0:T(8,128)(2,1)S(1)} %pad_maximum_fusion.pair_ref), channel_id=1, source_target_pairs={{2,0},{4,2},{6,4},{8,6},{10,8},{12,10},{14,12},{16,14},{18,16},{20... | collective-permute-start | bytes 393224 | tf_op jit(solution)/shard_map/ppermute | solution.py:224
  32.7 7.4 %collective-permute-start.8 = (bf16[2,64,512]{2,1,0:T(8,128)(2,1)S(1)}, bf16[2,64,512]{2,1,0:T(8,128)(2,1)S(1)}, u32[]{:S(2)}, u32[]{:S(2)}) collective-permute-start(bf16[2,64,512]{2,1,0:T(8,128)(2,1)S(1)} %collective-permute-done.4.refs_3_), channel_id=1, source_target_pairs={{0,1},{1,0},{2,3},{3,2},{4,5},{5,4},{6,7},{7,6},{8,9},{9,8},{10,11... | collective-permute-start | bytes 393224 | tf_op jit(solution)/shard_map/ppermute | solution.py:226
  35.8 4.3 %collective-permute-start.7 = (bf16[2,64,512]{2,1,0:T(8,128)(2,1)S(1)}, bf16[2,64,512]{2,1,0:T(8,128)(2,1)S(1)}, u32[]{:S(2)}, u32[]{:S(2)}) collective-permute-start(bf16[2,64,512]{2,1,0:T(8,128)(2,1)S(1)} %collective-permute-done.3.refs_2_), channel_id=1, source_target_pairs={{0,1},{1,0},{2,3},{3,2},{4,5},{5,4},{6,7},{7,6},{8,9},{9,8},{10,11... | collective-permute-start | bytes 393224 | tf_op jit(solution)/shard_map/ppermute | solution.py:226
  37.0 3.1 %collective-permute-start.6 = (bf16[2,64,512]{2,1,0:T(8,128)(2,1)S(1)}, bf16[2,64,512]{2,1,0:T(8,128)(2,1)S(1)}, u32[]{:S(2)}, u32[]{:S(2)}) collective-permute-start(bf16[2,64,512]{2,1,0:T(8,128)(2,1)S(1)} %collective-permute-done.2.refs_1_), channel_id=1, source_target_pairs={{0,1},{1,0},{2,3},{3,2},{4,5},{5,4},{6,7},{7,6},{8,9},{9,8},{10,11... | collective-permute-start | bytes 393224 | tf_op jit(solution)/shard_map/ppermute | solution.py:226
  40.2 1.3 %collective-permute-start.5 = (bf16[2,64,512]{2,1,0:T(8,128)(2,1)S(1)}, bf16[2,64,512]{2,1,0:T(8,128)(2,1)S(1)}, u32[]{:S(2)}, u32[]{:S(2)}) collective-permute-start(bf16[2,64,512]{2,1,0:T(8,128)(2,1)S(1)} %collective-permute-done.1.refs_0_), channel_id=1, source_target_pairs={{0,1},{1,0},{2,3},{3,2},{4,5},{5,4},{6,7},{7,6},{8,9},{9,8},{10,11... | collective-permute-start | bytes 393224 | tf_op jit(solution)/shard_map/ppermute | solution.py:226
  41.5 4.6 %copy-start = (f32[512,6144]{1,0:T(8,128)S(1)}, f32[512,6144]{1,0:T(8,128)}, u32[]{:S(2)}) copy-start(f32[512,6144]{1,0:T(8,128)} %blocks_ref.1) | copy-start | bytes 37748740
  53.4 2.2 %copy-start.2 = (bf16[512,128,32]{1,2,0:T(8,128)(2,1)S(1)}, bf16[512,128,32]{1,2,0:T(8,128)(2,1)}, u32[]{:S(2)}) copy-start(bf16[512,128,32]{1,2,0:T(8,128)(2,1)} %param.9) | copy-start | bytes 12582916

commit v2 on v0

v2 whole, which is shorter than its diff:
```python
import jax
import jax.numpy as jnp
from jax import lax
from jax.experimental import pallas as pl
from jax.experimental.pallas import tpu as pltpu
from jax.sharding import PartitionSpec as P

GROUP = 6

bf16 = jnp.bfloat16
f32 = jnp.float32
MiB = 2**20

SMEM = pl.BlockSpec(memory_space=pltpu.SMEM)
VMEM = pl.BlockSpec(memory_space=pltpu.VMEM)
HBM = pl.BlockSpec(memory_space=pltpu.HBM)


def start_all(copies):
    for copy in copies:
        copy.start()


def project_kernel(x_hbm, v_hbm, out_ref, source_ref, x_ref, raw_ref, turned_ref, small, sems):
    rank_max, rows, strips = turned_ref.shape
    sides = source_ref.shape[0]
    parts, pieces = sems.shape
    half = rank_max // parts
    chunk = rows // pieces
    first = pltpu.make_async_copy(x_hbm, x_ref, small)
    copies = [
        [
            pltpu.make_async_copy(
                v_hbm.at[pl.ds(n * chunk, chunk), pl.ds(h * half, half)],
                raw_ref.at[h, pl.ds(n * chunk, chunk)],
                sems.at[h, n],
            )
            for n in range(pieces)
        ]
        for h in range(parts)
    ]
    first.start()
    for part in copies:
        start_all(part)
    first.wait()
    source = x_ref[...].astype(bf16)
    source_ref[...] = source
    for h, part in enumerate(copies):
        for n, copy in enumerate(part):
            copy.wait()
            turned_ref[pl.ds(h * half, half), pl.ds(n * chunk, chunk), :] = jnp.swapaxes(
                raw_ref[h, pl.ds(n * chunk, chunk)], 0, 1
            )
        factors = jnp.concatenate([turned_ref[h * half + k] for k in range(half)], axis=1)
        product = jnp.dot(source, factors, preferred_element_type=f32)
        for k in range(half):
            place = pl.ds(k % 2 * sides, sides)
            value = product[:, k * strips : (k + 1) * strips]
            out_ref[(h * half + k) // 2, place, :] = value.astype(bf16)


def project(source, v_far):
    rows, rank_max, strips = v_far.shape
    sides = source.shape[0]
    parts = 2
    return pl.pallas_call(
        project_kernel,
        in_specs=[HBM, HBM],
        out_specs=[VMEM, VMEM],
        out_shape=[
            jax.ShapeDtypeStruct((rank_max // 2, 2 * sides, strips), bf16),
            jax.ShapeDtypeStruct(source.shape, bf16),
        ],
        scratch_shapes=[
            pltpu.VMEM(source.shape, f32),
            pltpu.VMEM((parts, rows, rank_max // parts, strips), bf16),
            pltpu.VMEM((rank_max, rows, strips), bf16),
            pltpu.SemaphoreType.DMA(()),
            pltpu.SemaphoreType.DMA((parts, 2)),
        ],
        compiler_params=pltpu.CompilerParams(vmem_limit_bytes=50 * MiB),
        cost_estimate=pl.CostEstimate(
            flops=2 * rows * rank_max * strips * sides,
            bytes_accessed=2 * rows * rank_max * strips,
            transcendentals=0,
        ),
        name="project",
    )(source, v_far)


def order_kernel(raw_ref, out_ref):
    turned = jnp.stack([raw_ref[p].T for p in range(raw_ref.shape[0])])
    out_ref[...] = jnp.swapaxes(turned, 0, 1)


def order(raw):
    pairs, width, strips = raw.shape
    return pl.pallas_call(
        order_kernel,
        in_specs=[VMEM],
        out_specs=VMEM,
        out_shape=jax.ShapeDtypeStruct((strips, pairs, width), bf16),
        compiler_params=pltpu.CompilerParams(vmem_limit_bytes=4 * MiB),
        cost_estimate=pl.CostEstimate(
            flops=0, bytes_accessed=4 * pairs * width * strips, transcendentals=0
        ),
        name="order",
    )(raw)


def group_kernel(me_ref, own_ref, sibling_ref, first_ref, second_ref, other_first_ref, other_second_ref, out_ref):
    core = me_ref[0] % 2
    out_ref[2 + core] = own_ref[...]
    out_ref[3 - core] = sibling_ref[...].astype(bf16)
    out_ref[4 - 3 * core] = first_ref[...].astype(bf16)
    out_ref[1 + 3 * core] = other_first_ref[...].astype(bf16)
    out_ref[5 * core] = second_ref[...].astype(bf16)
    out_ref[5 - 5 * core] = other_second_ref[...].astype(bf16)


def group(me, own, *others):
    return pl.pallas_call(
        group_kernel,
        in_specs=[SMEM] + [VMEM] * 6,
        out_specs=VMEM,
        out_shape=jax.ShapeDtypeStruct((GROUP, *own.shape), bf16),
        compiler_params=pltpu.CompilerParams(vmem_limit_bytes=4 * MiB),
        name="group",
    )(me, own, *others)


def near_kernel(me_ref, list_ref, count_ref, blocks_hbm, ranks_ref, own_ref, direct_ref, swapped_ref, out_ref, rank_ref, table_ref, gathered_ref, tiles_ref, sems):
    slots = list_ref.shape[0]
    parts, chunk, columns = tiles_ref.shape
    rows = columns // slots
    copies = [
        pltpu.make_async_copy(blocks_hbm.at[pl.ds(n * chunk, chunk)], tiles_ref.at[n], sems.at[n])
        for n in range(parts)
    ]
    start_all(copies)
    me = me_ref[0]
    core = me % 2
    strips, width = rank_ref.shape
    hot = (lax.broadcasted_iota(jnp.int32, (strips, width), 0) == me).astype(bf16)
    rank = lax.dot_general(
        ranks_ref[...].astype(f32).astype(bf16),
        hot,
        (((0,), (0,)), ((), ())),
        preferred_element_type=f32,
    )
    odd = lax.broadcasted_iota(jnp.int32, (strips, width), 1) >= out_ref.shape[0]
    rank_ref[...] = (rank - odd.astype(f32)).astype(bf16)
    table_ref[pl.ds(GROUP, GROUP)] = own_ref[...]
    table_ref[pl.ds(2 * GROUP * (1 - core), GROUP)] = direct_ref[...]
    table_ref[pl.ds(2 * GROUP * core, GROUP)] = swapped_ref[...]
    pair = me // 2
    above = jnp.where(pair == list_ref.shape[1] // 2 - 3, pair + 1, pair + 3)
    below = jnp.where(pair == 2, 1, pair - 3)
    for s in range(slots):
        strip = list_ref[s, me]
        side = strip // 2 - pair
        middle = jnp.where(side > 1, above, jnp.where(side < -1, below, pair))
        start = jnp.where(side > 1, 2 * GROUP, jnp.where(side < -1, 0, GROUP))
        place = start + jnp.clip(strip - 2 * (middle - 1), 0, GROUP - 1)
        value = table_ref[place]
        value = jnp.where(s < count_ref[me], value, jnp.zeros_like(value))
        gathered_ref[pl.ds(s * rows, rows), :] = value.T
    for n in range(parts):
        copies[n].wait()
        total = jnp.zeros((2 * chunk, out_ref.shape[0]), f32)
        for s in range(slots):
            tile = tiles_ref[n, :, pl.ds(s * rows, rows)]
            high = tile.astype(bf16)
            low = (tile - high.astype(f32)).astype(bf16)
            total += jnp.dot(
                jnp.concatenate([high, low], axis=0),
                gathered_ref[pl.ds(s * rows, rows), :],
                preferred_element_type=f32,
            )
        out_ref[:, pl.ds(n * chunk, chunk)] = (total[:chunk] + total[chunk:]).T


def near(me, near_list, near_count, near_blocks, ranks, own, direct, swapped):
    rows, columns = near_blocks.shape
    sides = own.shape[1]
    parts = 4
    return pl.pallas_call(
        near_kernel,
        in_specs=[SMEM, SMEM, SMEM, HBM, VMEM, VMEM, VMEM, VMEM],
        out_specs=[VMEM, VMEM],
        out_shape=[
            jax.ShapeDtypeStruct((sides, rows), f32),
            jax.ShapeDtypeStruct((ranks.shape[0], 2 * sides), bf16),
        ],
        scratch_shapes=[
            pltpu.VMEM((3 * GROUP, sides, rows), bf16),
            pltpu.VMEM((columns, sides), bf16),
            pltpu.VMEM((parts, rows // parts, columns), f32),
            pltpu.SemaphoreType.DMA((parts,)),
        ],
        compiler_params=pltpu.CompilerParams(vmem_limit_bytes=52 * MiB),
        cost_estimate=pl.CostEstimate(
            flops=4 * rows * columns * sides,
            bytes_accessed=4 * rows * columns,
            transcendentals=0,
        ),
        name="near",
    )(me, near_list.T, near_count, near_blocks, ranks, own, direct, swapped)


def far_kernel(near_ref, rank_ref, u_ref, coefficients_ref, out_ref, turned_ref):
    rows, rank_max, strips = u_ref.shape
    sides = out_ref.shape[0]
    turned_ref[...] = jnp.swapaxes(u_ref[...], 0, 1)
    rank = rank_ref[...]
    turned = jnp.swapaxes(coefficients_ref[...], 0, 1)
    weights = []
    for p in range(rank_max // 2):
        kept = jnp.where(rank > 2 * p, turned[p], jnp.zeros_like(turned[p]))
        weights += [kept[:, :sides], kept[:, sides:]]
    weights = jnp.concatenate(weights, axis=0)
    factors = jnp.concatenate([turned_ref[k] for k in range(rank_max)], axis=1)
    far = jnp.dot(factors, weights, preferred_element_type=f32)
    out_ref[...] = near_ref[...] + far.T


def add_far(near_field, rank, u_far, coefficients):
    rows, rank_max, strips = u_far.shape
    sides = near_field.shape[0]
    return pl.pallas_call(
        far_kernel,
        in_specs=[VMEM, VMEM, VMEM, VMEM],
        out_specs=VMEM,
        out_shape=jax.ShapeDtypeStruct((sides, rows), f32),
        scratch_shapes=[pltpu.VMEM((rank_max, rows, strips), bf16)],
        compiler_params=pltpu.CompilerParams(vmem_limit_bytes=16 * MiB),
        cost_estimate=pl.CostEstimate(
            flops=2 * rows * rank_max * strips * sides,
            bytes_accessed=2 * rows * rank_max * strips,
            transcendentals=0,
        ),
        name="add_far",
    )(near_field, rank, u_far, coefficients)


def exchanges(strips):
    pairs = strips // 2
    sibling = [(d, d ^ 1) for d in range(strips)]
    first = [(2 * c + 2, 2 * c) for c in range(pairs - 1)] + [(0, 1)]
    first += [(2 * c + 1, 2 * c + 3) for c in range(pairs - 1)] + [(strips - 1, strips - 2)]
    second = [(b, a) for a, b in first]
    groups = [(2 * (c + 3), 2 * c) for c in range(pairs - 3)]
    groups += [(2 * c + 1, 2 * (c + 3) + 1) for c in range(pairs - 3)]
    groups += [(2, 5), (4, 3), (0, 1)]
    groups += [(strips - 1 - a, strips - 1 - b) for a, b in ((2, 5), (4, 3), (0, 1))]
    return sibling, first, second, groups


def body(density, near_blocks, u_far, v_far, ranks, near_list, near_count):
    me = lax.axis_index("strip").astype(jnp.int32).reshape(1)
    sibling, first, second, groups = exchanges(lax.axis_size("strip"))
    source = density.T
    held = [lax.ppermute(source, "strip", moves) for moves in (sibling, first, second)]
    raw, source_bf = project(source, jnp.transpose(v_far, (0, 2, 1)))
    raw, *held[1:] = lax.optimization_barrier((raw, *held[1:]))
    held += [lax.ppermute(strip, "strip", sibling) for strip in held[1:]]
    own = group(me, source_bf, *held)
    raw, own = lax.optimization_barrier((raw, own))
    direct = lax.ppermute(own, "strip", groups)
    outgoing = order(raw)
    incoming = lax.all_to_all(outgoing, "strip", split_axis=0, concat_axis=0, tiled=True)
    swapped = lax.ppermute(direct, "strip", sibling)
    near_field, rank = near(me, near_list, near_count, near_blocks, ranks, own, direct, swapped)
    return add_far(near_field, rank, jnp.transpose(u_far, (0, 2, 1)), incoming).T


def solution(mesh):
    return jax.shard_map(
        body,
        mesh=mesh,
        in_specs=(
            P("strip", None),
            P("strip", None),
            P("strip", None, None),
            P("strip", None, None),
            P(),
            P(),
            P(),
        ),
        out_specs=P("strip", None),
        check_vma=False,
    )
```

time: 128 us -> 44.6 us (0.35)
  the two profiles are of different devices: /device:TPU:59 before, /device:TPU:1 now
where the time goes in v2:
time: 44.6 us; the launch traced here: 44.4 us
  starting transfers between devices  20 us (45%)
  Pallas kernels  14.5 us (33%)
  waiting for transfers between devices  6.78 us (15%)
  local copies, waits for them, and re-layouts  3.1 us (7%)
    all_to_all x1, starting transfers between devices, body(): lax.all_to_all(outgoing, 'strip', split_axis=0, concat_axis=0, tiled=True)  10.5 us
    pallas_call x1, Pallas kernels, near(): pl.pallas_call(near_kernel, in_specs=[SMEM, SMEM, SMEM, HBM, VMEM, VMEM,...  7.12 us
    ppermute x1, starting transfers between devices, body(): direct = lax.ppermute(own, 'strip', groups)  4.66 us
    all_to_all x1, waiting for transfers between devices, body(): lax.all_to_all(outgoing, 'strip', split_axis=0, concat_axis=0, tiled=True)  4.08 us
    pallas_call x1, Pallas kernels, project(): pl.pallas_call(project_kernel, in_specs=[HBM, HBM], out_specs=[VMEM, VMEM...  3.56 us
    unnamed x10, local copies, waits for them, and re-layouts  3.1 us
    ppermute x3, starting transfers between devices, body(): lax.ppermute(source, 'strip', moves)  3 us
    pallas_call x1, Pallas kernels, add_far(): pl.pallas_call(far_kernel, in_specs=[VMEM, VMEM, VMEM, VMEM], out_specs=V...  2.8 us
  transfers between devices with their start and end apart: 8, of which 4 were waited for; matrix products, arithmetic and copies ran while one was open for 0% of the time, Pallas kernels for 26%

profile of v2, /device:TPU:1, one launch (start us, length us, event | category | flops | bytes accessed | tf_op | source)
XLA Modules:
  0.0 44.4 jit_solution(9869485491287440605)
XLA Ops:
  0.0 0.0 copy-start.4
  0.0 1.4 %collective-permute-start.1 = (f32[64,512]{1,0:T(8,128)}, f32[64,512]{1,0:T(8,128)S(1)}, u32[]{:S(2)}, u32[]{:S(2)}) collective-permute-start(f32[64,512]{1,0:T(8,128)} %bitcast.7), channel_id=1, source_target_pairs={{0,2},{2,4},{4,6},{6,8},{8,10},{10,12},{12,14},{14,16},{16,18},{18... | collective-permute-start | bytes 393224 | tf_op jit(solution)/shard_map/ppermute | solution.py:263
  1.4 0.7 %collective-permute-start = (f32[64,512]{1,0:T(8,128)}, f32[64,512]{1,0:T(8,128)S(1)}, u32[]{:S(2)}, u32[]{:S(2)}) collective-permute-start(f32[64,512]{1,0:T(8,128)} %bitcast.8), channel_id=1, source_target_pairs={{2,0},{4,2},{6,4},{8,6},{10,8},{12,10},{14,12},{16,14},{18,16},{20... | collective-permute-start | bytes 393224 | tf_op jit(solution)/shard_map/ppermute | solution.py:263
  2.1 0.9 %collective-permute-start.2 = (f32[64,512]{1,0:T(8,128)}, f32[64,512]{1,0:T(8,128)S(1)}, u32[]{:S(2)}, u32[]{:S(2)}) collective-permute-start(f32[64,512]{1,0:T(8,128)} %bitcast.9), channel_id=1, source_target_pairs={{0,1},{1,0},{2,3},{3,2},{4,5},{5,4},{6,7},{7,6},{8,9},{9,8},{10,11... | collective-permute-start | bytes 393224 | tf_op jit(solution)/shard_map/ppermute | solution.py:263
  3.0 0.0 copy-start.1
  3.0 0.9 %copy-done.1 = f32[512,64]{0,1:T(8,128)S(1)} copy-done((f32[512,64]{0,1:T(8,128)S(1)}, f32[512,64]{0,1:T(8,128)}, u32[]{:S(2)}) %copy-start.1) | copy-done | bytes 131096
  3.9 0.0 copy-start.2
  3.9 0.0 copy-start.3
  3.9 3.6 %project.1 = (bf16[16,128,128]{2,1,0:T(8,128)(2,1)S(1)}, bf16[64,512]{1,0:T(8,128)(2,1)S(1)}) custom-call(f32[64,512]{1,0:T(8,128)S(1)} %bitcast.10, bf16[512,32,128]{2,1,0:T(8,128)(2,1)} %bitcast.12), custom_call_target="tpu_custom_call" | custom-call | flops 268435456 | bytes 4194304 | tf_op jit(solution)/shard_map/project/pallas_call | solution.py:66
  7.5 0.0 collective-permute-done.1.second_ref
  7.5 0.0 collective-permute-done.first_ref
  7.5 0.7 %collective-permute-start.3 = (f32[64,512]{1,0:T(8,128)S(1)}, f32[64,512]{1,0:T(8,128)S(1)}, u32[]{:S(2)}, u32[]{:S(2)}) collective-permute-start(f32[64,512]{1,0:T(8,128)S(1)} %collective-permute-done.first_ref), channel_id=1, source_target_pairs={{0,1},{1,0},{2,3},{3,2},{4,5},{5,4},{6,7},{7,6},{8,9},{9,8},{10,11... | collective-permute-start | bytes 393224 | tf_op jit(solution)/shard_map/ppermute | solution.py:266
  8.2 0.0 collective-permute-start.4
  8.2 0.0 collective-permute-done.2.sibling_ref
  8.2 1.0 %collective-permute-done.3.other_first_ref = f32[64,512]{1,0:T(8,128)S(1)} collective-permute-done((f32[64,512]{1,0:T(8,128)S(1)}, f32[64,512]{1,0:T(8,128)S(1)}, u32[]{:S(2)}, u32[]{:S(2)}) %collective-permute-start.3) | collective-permute-done | bytes 131104 | tf_op jit(solution)/shard_map/ppermute | solution.py:266
  9.2 0.4 collective-permute-done.4.other_second_ref
  9.6 4.7 %collective-permute-start.5 = (bf16[6,64,512]{2,1,0:T(8,128)(2,1)S(1)}, bf16[6,64,512]{2,1,0:T(8,128)(2,1)S(1)}, u32[]{:S(2)}, u32[]{:S(2)}) collective-permute-start(bf16[6,64,512]{2,1,0:T(8,128)(2,1)S(1)} %group.1.own_ref), channel_id=1, source_target_pairs={{6,0},{8,2},{10,4},{12,6},{14,8},{16,10},{18,12},{20,14},{22,16},{... | collective-permute-start | bytes 1179656 | tf_op jit(solution)/shard_map/ppermute | solution.py:269
  14.2 1.0 %order.1 = bf16[128,16,128]{2,1,0:T(8,128)(2,1)} custom-call(bf16[16,128,128]{2,1,0:T(8,128)(2,1)S(1)} %get-tuple-element.22.raw_ref), custom_call_target="tpu_custom_call" | custom-call | bytes 1048576 | tf_op jit(solution)/shard_map/order/pallas_call | solution.py:98
  15.2 10.5 %all-to-all-start = ((bf16[128,16,128]{2,1,0:T(8,128)(2,1)}), bf16[128,16,128]{2,1,0:T(8,128)(2,1)S(1)}, u32[]{:S(2)}, u32[]{:S(2)}) async-start(bf16[128,16,128]{2,1,0:T(8,128)(2,1)} %order.1), calls=%async_computation | async-start | bytes 1048576 | tf_op jit(solution)/shard_map/all_to_all | solution.py:271
  25.7 0.0 collective-permute-done.5.direct_ref
  25.7 1.1 %collective-permute-start.6 = (bf16[6,64,512]{2,1,0:T(8,128)(2,1)S(1)}, bf16[6,64,512]{2,1,0:T(8,128)(2,1)S(1)}, u32[]{:S(2)}, u32[]{:S(2)}) collective-permute-start(bf16[6,64,512]{2,1,0:T(8,128)(2,1)S(1)} %collective-permute-done.5.direct_ref), channel_id=1, source_target_pairs={{0,1},{1,0},{2,3},{3,2},{4,5},{5,4},{6,7},{7,6},{8,9},{9,8},{10,11... | collective-permute-start | bytes 1179656 | tf_op jit(solution)/shard_map/ppermute | solution.py:272
  26.9 1.3 %collective-permute-done.6.swapped_ref = bf16[6,64,512]{2,1,0:T(8,128)(2,1)S(1)} collective-permute-done((bf16[6,64,512]{2,1,0:T(8,128)(2,1)S(1)}, bf16[6,64,512]{2,1,0:T(8,128)(2,1)S(1)}, u32[]{:S(2)}, u32[]{:S(2)}) %collective-permute-start.6) | collective-permute-done | bytes 393248 | tf_op jit(solution)/shard_map/ppermute | solution.py:272
  28.2 0.0 copy-done.4
  28.2 0.0 copy-done.2
  28.2 0.0 copy-done.3
  28.2 7.1 %near.1 = (f32[64,512]{1,0:T(8,128)S(1)}, bf16[128,128]{1,0:T(8,128)(2,1)S(1)}) custom-call(s32[1]{0:T(128)} %bitcast.me_ref, s32[12,128]{1,0:T(8,128)S(1)} %bitcast.11, s32[128]{0:T(128)S(1)} %copy-done.4, f32[512,6144]{1,0:T(8,128)} %blocks_hbm.1, s32[128,128]{1,0:T(8,128)S(1)} %copy-done.2, bf16[6,64,512]{2,1,0:T(8,128)(2,1)S(1)} %group.1.own_ref, ...), custom_call_target="tpu_custom_call" | custom-call | flops 805306368 | bytes 12582912 | tf_op jit(solution)/shard_map/near/pallas_call | solution.py:187
  35.4 4.1 %all-to-all-done.coefficients_ref = bf16[128,16,128]{2,1,0:T(8,128)(2,1)S(1)} async-done(((bf16[128,16,128]{2,1,0:T(8,128)(2,1)}), bf16[128,16,128]{2,1,0:T(8,128)(2,1)S(1)}, u32[]{:S(2)}, u32[]{:S(2)}) %all-to-all-start) | async-done | bytes 524320 | tf_op jit(solution)/shard_map/all_to_all | solution.py:271
  39.4 0.0 copy-start
  39.4 2.2 %copy-done = bf16[512,128,32]{1,2,0:T(8,128)(2,1)S(1)} copy-done((bf16[512,128,32]{1,2,0:T(8,128)(2,1)S(1)}, bf16[512,128,32]{1,2,0:T(8,128)(2,1)}, u32[]{:S(2)}) %copy-start) | copy-done | bytes 4194328
  41.6 2.8 %add_far.1 = f32[64,512]{1,0:T(8,128)} custom-call(f32[64,512]{1,0:T(8,128)S(1)} %get-tuple-element.20.near_ref, bf16[128,128]{1,0:T(8,128)(2,1)S(1)} %get-tuple-element.21.rank_ref, bf16[512,32,128]{2,1,0:T(8,128)(2,1)S(1)} %bitcast.6, bf16[128,16,128]{2,1,0:T(8,128)(2,1)S(1)} %all-to-all-done.coefficients_ref), custom_call_target="tpu_custom_call" | custom-call | flops 268435456 | bytes 4194304 | tf_op jit(solution)/shard_map/add_far/pallas_call | solution.py:230
  (1 shorter events, 0.0 us)
Async XLA Ops:
  0.0 28.2 %copy-start.4 = (s32[128]{0:T(128)S(1)}, s32[128]{0:T(128)}, u32[]{:S(2)}) copy-start(s32[128]{0:T(128)} %count_ref.1) | copy-start | bytes 1540
  0.0 7.5 %collective-permute-start.1 = (f32[64,512]{1,0:T(8,128)}, f32[64,512]{1,0:T(8,128)S(1)}, u32[]{:S(2)}, u32[]{:S(2)}) collective-permute-start(f32[64,512]{1,0:T(8,128)} %bitcast.7), channel_id=1, source_target_pairs={{0,2},{2,4},{4,6},{6,8},{8,10},{10,12},{12,14},{14,16},{16,18},{18... | collective-permute-start | bytes 393224 | tf_op jit(solution)/shard_map/ppermute | solution.py:263
  1.4 6.1 %collective-permute-start = (f32[64,512]{1,0:T(8,128)}, f32[64,512]{1,0:T(8,128)S(1)}, u32[]{:S(2)}, u32[]{:S(2)}) collective-permute-start(f32[64,512]{1,0:T(8,128)} %bitcast.8), channel_id=1, source_target_pairs={{2,0},{4,2},{6,4},{8,6},{10,8},{12,10},{14,12},{16,14},{18,16},{20... | collective-permute-start | bytes 393224 | tf_op jit(solution)/shard_map/ppermute | solution.py:263
  2.1 6.1 %collective-permute-start.2 = (f32[64,512]{1,0:T(8,128)}, f32[64,512]{1,0:T(8,128)S(1)}, u32[]{:S(2)}, u32[]{:S(2)}) collective-permute-start(f32[64,512]{1,0:T(8,128)} %bitcast.9), channel_id=1, source_target_pairs={{0,1},{1,0},{2,3},{3,2},{4,5},{5,4},{6,7},{7,6},{8,9},{9,8},{10,11... | collective-permute-start | bytes 393224 | tf_op jit(solution)/shard_map/ppermute | solution.py:263
  3.0 0.9 %copy-start.1 = (f32[512,64]{0,1:T(8,128)S(1)}, f32[512,64]{0,1:T(8,128)}, u32[]{:S(2)}) copy-start(f32[512,64]{0,1:T(8,128)} %param.7) | copy-start | bytes 393220
  3.9 24.3 %copy-start.2 = (s32[128,128]{1,0:T(8,128)S(1)}, s32[128,128]{1,0:T(8,128)}, u32[]{:S(2)}) copy-start(s32[128,128]{1,0:T(8,128)} %ranks_ref.1) | copy-start | bytes 196612
  3.9 24.3 %copy-start.3 = (s32[128,12]{0,1:T(8,128)S(1)}, s32[128,12]{0,1:T(8,128)}, u32[]{:S(2)}) copy-start(s32[128,12]{0,1:T(8,128)} %param.12) | copy-start | bytes 18436
  7.5 1.7 %collective-permute-start.3 = (f32[64,512]{1,0:T(8,128)S(1)}, f32[64,512]{1,0:T(8,128)S(1)}, u32[]{:S(2)}, u32[]{:S(2)}) collective-permute-start(f32[64,512]{1,0:T(8,128)S(1)} %collective-permute-done.first_ref), channel_id=1, source_target_pairs={{0,1},{1,0},{2,3},{3,2},{4,5},{5,4},{6,7},{7,6},{8,9},{9,8},{10,11... | collective-permute-start | bytes 393224 | tf_op jit(solution)/shard_map/ppermute | solution.py:266
  8.2 1.3 %collective-permute-start.4 = (f32[64,512]{1,0:T(8,128)S(1)}, f32[64,512]{1,0:T(8,128)S(1)}, u32[]{:S(2)}, u32[]{:S(2)}) collective-permute-start(f32[64,512]{1,0:T(8,128)S(1)} %collective-permute-done.1.second_ref), channel_id=1, source_target_pairs={{0,1},{1,0},{2,3},{3,2},{4,5},{5,4},{6,7},{7,6},{8,9},{9,8},{10,11... | collective-permute-start | bytes 393224 | tf_op jit(solution)/shard_map/ppermute | solution.py:266
  9.6 16.1 %collective-permute-start.5 = (bf16[6,64,512]{2,1,0:T(8,128)(2,1)S(1)}, bf16[6,64,512]{2,1,0:T(8,128)(2,1)S(1)}, u32[]{:S(2)}, u32[]{:S(2)}) collective-permute-start(bf16[6,64,512]{2,1,0:T(8,128)(2,1)S(1)} %group.1.own_ref), channel_id=1, source_target_pairs={{6,0},{8,2},{10,4},{12,6},{14,8},{16,10},{18,12},{20,14},{22,16},{... | collective-permute-start | bytes 1179656 | tf_op jit(solution)/shard_map/ppermute | solution.py:269
  15.2 24.2 %all-to-all-start = ((bf16[128,16,128]{2,1,0:T(8,128)(2,1)}), bf16[128,16,128]{2,1,0:T(8,128)(2,1)S(1)}, u32[]{:S(2)}, u32[]{:S(2)}) async-start(bf16[128,16,128]{2,1,0:T(8,128)(2,1)} %order.1), calls=%async_computation | async-start | bytes 1048576 | tf_op jit(solution)/shard_map/all_to_all | solution.py:271
  25.7 2.5 %collective-permute-start.6 = (bf16[6,64,512]{2,1,0:T(8,128)(2,1)S(1)}, bf16[6,64,512]{2,1,0:T(8,128)(2,1)S(1)}, u32[]{:S(2)}, u32[]{:S(2)}) collective-permute-start(bf16[6,64,512]{2,1,0:T(8,128)(2,1)S(1)} %collective-permute-done.5.direct_ref), channel_id=1, source_target_pairs={{0,1},{1,0},{2,3},{3,2},{4,5},{5,4},{6,7},{7,6},{8,9},{9,8},{10,11... | collective-permute-start | bytes 1179656 | tf_op jit(solution)/shard_map/ppermute | solution.py:272
  39.4 2.2 %copy-start = (bf16[512,128,32]{1,2,0:T(8,128)(2,1)S(1)}, bf16[512,128,32]{1,2,0:T(8,128)(2,1)}, u32[]{:S(2)}) copy-start(bf16[512,128,32]{1,2,0:T(8,128)(2,1)} %param.9) | copy-start | bytes 12582916

commit v3 on v2

--- a/solution.py
+++ b/solution.py
@@ -21,33 +21,18 @@
         copy.start()
 
 
-def project_kernel(x_hbm, v_hbm, out_ref, source_ref, x_ref, raw_ref, turned_ref, small, sems):
+def project_kernel(pair_ref, v_hbm, out_ref, raw_ref, turned_ref, sems):
     rank_max, rows, strips = turned_ref.shape
-    sides = source_ref.shape[0]
+    sides = pair_ref.shape[1]
     parts, pieces = sems.shape
     half = rank_max // parts
     chunk = rows // pieces
-    first = pltpu.make_async_copy(x_hbm, x_ref, small)
-    copies = [
-        [
-            pltpu.make_async_copy(
-                v_hbm.at[pl.ds(n * chunk, chunk), pl.ds(h * half, half)],
-                raw_ref.at[h, pl.ds(n * chunk, chunk)],
-                sems.at[h, n],
-            )
-            for n in range(pieces)
-        ]
-        for h in range(parts)
-    ]
-    first.start()
-    for part in copies:
-        start_all(part)
-    first.wait()
-    source = x_ref[...].astype(bf16)
-    source_ref[...] = source
-    for h, part in enumerate(copies):
-        for n, copy in enumerate(part):
-            copy.wait()
+    copies = staged_copies(v_hbm, raw_ref, sems)
+    start_all(copies)
+    source = pair_ref[0]
+    for h in range(parts):
+        for n in range(pieces):
+            copies[h * pieces + n].wait()
             turned_ref[pl.ds(h * half, half), pl.ds(n * chunk, chunk), :] = jnp.swapaxes(
                 raw_ref[h, pl.ds(n * chunk, chunk)], 0, 1
             )
@@ -59,33 +44,28 @@
             out_ref[(h * half + k) // 2, place, :] = value.astype(bf16)
 
 
-def project(source, v_far):
+def project(pair, v_far):
     rows, rank_max, strips = v_far.shape
-    sides = source.shape[0]
+    sides = pair.shape[1]
     parts = 2
     return pl.pallas_call(
         project_kernel,
-        in_specs=[HBM, HBM],
-        out_specs=[VMEM, VMEM],
-        out_shape=[
-            jax.ShapeDtypeStruct((rank_max // 2, 2 * sides, strips), bf16),
-            jax.ShapeDtypeStruct(source.shape, bf16),
-        ],
+        in_specs=[VMEM, HBM],
+        out_specs=VMEM,
+        out_shape=jax.ShapeDtypeStruct((rank_max // 2, 2 * sides, strips), bf16),
         scratch_shapes=[
-            pltpu.VMEM(source.shape, f32),
             pltpu.VMEM((parts, rows, rank_max // parts, strips), bf16),
             pltpu.VMEM((rank_max, rows, strips), bf16),
-            pltpu.SemaphoreType.DMA(()),
-            pltpu.SemaphoreType.DMA((parts, 2)),
+            pltpu.SemaphoreType.DMA((parts, 4)),
         ],
-        compiler_params=pltpu.CompilerParams(vmem_limit_bytes=50 * MiB),
+        compiler_params=pltpu.CompilerParams(vmem_limit_bytes=53 * MiB),
         cost_estimate=pl.CostEstimate(
             flops=2 * rows * rank_max * strips * sides,
             bytes_accessed=2 * rows * rank_max * strips,
             transcendentals=0,
         ),
         name="project",
-    )(source, v_far)
+    )(pair, v_far)
 
 
 def order_kernel(raw_ref, out_ref):
@@ -108,25 +88,69 @@
     )(raw)
 
 
-def group_kernel(me_ref, own_ref, sibling_ref, first_ref, second_ref, other_first_ref, other_second_ref, out_ref):
+def staged_copies(source_hbm, raw_ref, sems):
+    half = raw_ref.shape[2]
+    parts, pieces = sems.shape
+    chunk = raw_ref.shape[1] // pieces
+    return [
+        pltpu.make_async_copy(
+            source_hbm.at[pl.ds(n * chunk, chunk), pl.ds(h * half, half)],
+            raw_ref.at[h, pl.ds(n * chunk, chunk)],
+            sems.at[h, n],
+        )
+        for h in range(parts)
+        for n in range(pieces)
+    ]
+
+
+def cast_kernel(in_ref, out_ref):
+    out_ref[...] = in_ref[...].astype(bf16)
+
+
+def cast(value):
+    return pl.pallas_call(
+        cast_kernel,
+        in_specs=[VMEM],
+        out_specs=VMEM,
+        out_shape=jax.ShapeDtypeStruct(value.shape, bf16),
+        compiler_params=pltpu.CompilerParams(vmem_limit_bytes=2 * MiB),
+        name="cast",
+    )(value)
+
+
+def pack_kernel(own_ref, sibling_ref, out_ref):
+    out_ref[0] = own_ref[...]
+    out_ref[1] = sibling_ref[...].astype(bf16)
+
+
+def pack(own, sibling):
+    return pl.pallas_call(
+        pack_kernel,
+        in_specs=[VMEM, VMEM],
+        out_specs=VMEM,
+        out_shape=jax.ShapeDtypeStruct((2, *own.shape), bf16),
+        compiler_params=pltpu.CompilerParams(vmem_limit_bytes=2 * MiB),
+        name="pack",
+    )(own, sibling)
+
+
+def group_kernel(me_ref, pair_ref, next_ref, other_ref, out_ref):
     core = me_ref[0] % 2
-    out_ref[2 + core] = own_ref[...]
-    out_ref[3 - core] = sibling_ref[...].astype(bf16)
-    out_ref[4 - 3 * core] = first_ref[...].astype(bf16)
-    out_ref[1 + 3 * core] = other_first_ref[...].astype(bf16)
-    out_ref[5 * core] = second_ref[...].astype(bf16)
-    out_ref[5 - 5 * core] = other_second_ref[...].astype(bf16)
-
-
-def group(me, own, *others):
+    for n in range(2):
+        out_ref[2 + (core + n) % 2] = pair_ref[n]
+        out_ref[4 - 4 * core + (core + n) % 2] = next_ref[n]
+        out_ref[4 * core + (1 - core + n) % 2] = other_ref[n]
+
+
+def group(me, pair, following, other):
     return pl.pallas_call(
         group_kernel,
-        in_specs=[SMEM] + [VMEM] * 6,
-        out_specs=VMEM,
-        out_shape=jax.ShapeDtypeStruct((GROUP, *own.shape), bf16),
+        in_specs=[SMEM] + [VMEM] * 3,
+        out_specs=VMEM,
+        out_shape=jax.ShapeDtypeStruct((GROUP, *pair.shape[1:]), bf16),
         compiler_params=pltpu.CompilerParams(vmem_limit_bytes=4 * MiB),
         name="group",
-    )(me, own, *others)
+    )(me, pair, following, other)
 
 
 def near_kernel(me_ref, list_ref, count_ref, blocks_hbm, ranks_ref, own_ref, direct_ref, swapped_ref, out_ref, rank_ref, table_ref, gathered_ref, tiles_ref, sems):
@@ -208,32 +232,47 @@
     )(me, near_list.T, near_count, near_blocks, ranks, own, direct, swapped)
 
 
-def far_kernel(near_ref, rank_ref, u_ref, coefficients_ref, out_ref, turned_ref):
-    rows, rank_max, strips = u_ref.shape
+def far_kernel(near_ref, rank_ref, u_hbm, coefficients_ref, out_ref, raw_ref, turned_ref, sems):
+    parts, rows, half, strips = raw_ref.shape
     sides = out_ref.shape[0]
-    turned_ref[...] = jnp.swapaxes(u_ref[...], 0, 1)
+    pieces = sems.shape[1]
+    chunk = rows // pieces
+    copies = staged_copies(u_hbm, raw_ref, sems)
+    start_all(copies)
     rank = rank_ref[...]
     turned = jnp.swapaxes(coefficients_ref[...], 0, 1)
     weights = []
-    for p in range(rank_max // 2):
+    for p in range(parts * half // 2):
         kept = jnp.where(rank > 2 * p, turned[p], jnp.zeros_like(turned[p]))
         weights += [kept[:, :sides], kept[:, sides:]]
-    weights = jnp.concatenate(weights, axis=0)
-    factors = jnp.concatenate([turned_ref[k] for k in range(rank_max)], axis=1)
-    far = jnp.dot(factors, weights, preferred_element_type=f32)
+    far = jnp.zeros((rows, sides), f32)
+    for h in range(parts):
+        for n in range(pieces):
+            copies[h * pieces + n].wait()
+            part = pl.ds(n * chunk, chunk)
+            turned_ref[h, :, part, :] = jnp.swapaxes(raw_ref[h, part], 0, 1)
+        factors = jnp.concatenate([turned_ref[h, k] for k in range(half)], axis=1)
+        part = jnp.concatenate(weights[h * half : (h + 1) * half], axis=0)
+        far += jnp.dot(factors, part, preferred_element_type=f32)
     out_ref[...] = near_ref[...] + far.T
 
 
 def add_far(near_field, rank, u_far, coefficients):
     rows, rank_max, strips = u_far.shape
     sides = near_field.shape[0]
+    parts = 2
+    half = rank_max // parts
     return pl.pallas_call(
         far_kernel,
-        in_specs=[VMEM, VMEM, VMEM, VMEM],
+        in_specs=[VMEM, VMEM, HBM, VMEM],
         out_specs=VMEM,
         out_shape=jax.ShapeDtypeStruct((sides, rows), f32),
-        scratch_shapes=[pltpu.VMEM((rank_max, rows, strips), bf16)],
-        compiler_params=pltpu.CompilerParams(vmem_limit_bytes=16 * MiB),
+        scratch_shapes=[
+            pltpu.VMEM((parts, rows, half, strips), bf16),
+            pltpu.VMEM((parts, half, rows, strips), bf16),
+            pltpu.SemaphoreType.DMA((parts, 4)),
+        ],
+        compiler_params=pltpu.CompilerParams(vmem_limit_bytes=53 * MiB),
         cost_estimate=pl.CostEstimate(
             flops=2 * rows * rank_max * strips * sides,
             bytes_accessed=2 * rows * rank_max * strips,
@@ -246,28 +285,28 @@
 def exchanges(strips):
     pairs = strips // 2
     sibling = [(d, d ^ 1) for d in range(strips)]
-    first = [(2 * c + 2, 2 * c) for c in range(pairs - 1)] + [(0, 1)]
-    first += [(2 * c + 1, 2 * c + 3) for c in range(pairs - 1)] + [(strips - 1, strips - 2)]
-    second = [(b, a) for a, b in first]
+    following = [(2 * c + 2, 2 * c) for c in range(pairs - 1)] + [(0, 1)]
+    following += [(2 * c + 1, 2 * c + 3) for c in range(pairs - 1)] + [(strips - 1, strips - 2)]
     groups = [(2 * (c + 3), 2 * c) for c in range(pairs - 3)]
     groups += [(2 * c + 1, 2 * (c + 3) + 1) for c in range(pairs - 3)]
     groups += [(2, 5), (4, 3), (0, 1)]
     groups += [(strips - 1 - a, strips - 1 - b) for a, b in ((2, 5), (4, 3), (0, 1))]
-    return sibling, first, second, groups
+    return sibling, following, groups
 
 
 def body(density, near_blocks, u_far, v_far, ranks, near_list, near_count):
     me = lax.axis_index("strip").astype(jnp.int32).reshape(1)
-    sibling, first, second, groups = exchanges(lax.axis_size("strip"))
+    sibling, following, groups = exchanges(lax.axis_size("strip"))
     source = density.T
-    held = [lax.ppermute(source, "strip", moves) for moves in (sibling, first, second)]
-    raw, source_bf = project(source, jnp.transpose(v_far, (0, 2, 1)))
-    raw, *held[1:] = lax.optimization_barrier((raw, *held[1:]))
-    held += [lax.ppermute(strip, "strip", sibling) for strip in held[1:]]
-    own = group(me, source_bf, *held)
-    raw, own = lax.optimization_barrier((raw, own))
+    pair = pack(cast(source), lax.ppermute(source, "strip", sibling))
+    follower = lax.ppermute(pair, "strip", following)
+    raw = project(pair, jnp.transpose(v_far, (0, 2, 1)))
+    raw, follower = lax.optimization_barrier((raw, follower))
+    other = lax.ppermute(follower, "strip", sibling)
+    outgoing = order(raw)
+    outgoing, pair, follower, other = lax.optimization_barrier((outgoing, pair, follower, other))
+    own = group(me, pair, follower, other)
     direct = lax.ppermute(own, "strip", groups)
-    outgoing = order(raw)
     incoming = lax.all_to_all(outgoing, "strip", split_axis=0, concat_axis=0, tiled=True)
     swapped = lax.ppermute(direct, "strip", sibling)
     near_field, rank = near(me, near_list, near_count, near_blocks, ranks, own, direct, swapped)

time: 44.6 us -> 43.1 us (0.966)
  local copies, waits for them, and re-layouts: 3.1 us -> 0.91 us
  Pallas kernels: 14.5 us -> 16 us
  waiting for transfers between devices: 6.78 us -> 5.72 us
    unnamed x10 -> x8, local copies, waits for them, and re-layouts: 3.1 us -> 0.91 us
    pallas_call x3 -> x5, Pallas kernels: 6.4 us -> 7.86 us  [the longest x1 4.51 us: add_far(): pl.pallas_call(far_kernel, in_specs=[VMEM, VMEM, HBM, VMEM], out_specs=VM...]
    ppermute x5 -> x3, waiting for transfers between devices: 1.35 us -> 0.28 us  [the longest x1 0.28 us: body(): pair = pack(cast(source), lax.ppermute(source, 'strip', sibling))]
    ppermute x5 -> x3, starting transfers between devices: 3.68 us -> 3.51 us  [the longest x1 1.42 us: body(): pair = pack(cast(source), lax.ppermute(source, 'strip', sibling))]
  transfers between devices with their start and end apart: 8 -> 6, of which waited for: 4 -> 3; matrix products, arithmetic and copies ran while one was open for 0% -> 0% of each run, Pallas kernels for 26% -> 27%
where the time goes in v3:
time: 43.1 us; the launch traced here: 42.9 us
  starting transfers between devices  20.2 us (47%)
  Pallas kernels  16 us (37%)
  waiting for transfers between devices  5.72 us (13%)
  local copies, waits for them, and re-layouts  0.91 us (2%)
    all_to_all x1, starting transfers between devices, body(): lax.all_to_all(outgoing, 'strip', split_axis=0, concat_axis=0, tiled=True)  10.8 us
    pallas_call x1, Pallas kernels, near(): pl.pallas_call(near_kernel, in_specs=[SMEM, SMEM, SMEM, HBM, VMEM, VMEM,...  7.12 us
    ppermute x1, starting transfers between devices, body(): direct = lax.ppermute(own, 'strip', groups)  4.75 us
    pallas_call x1, Pallas kernels, add_far(): pl.pallas_call(far_kernel, in_specs=[VMEM, VMEM, HBM, VMEM], out_specs=VM...  4.51 us
    all_to_all x1, waiting for transfers between devices, body(): lax.all_to_all(outgoing, 'strip', split_axis=0, concat_axis=0, tiled=True)  4.08 us
    pallas_call x1, Pallas kernels, project(): pl.pallas_call(project_kernel, in_specs=[VMEM, HBM], out_specs=VMEM, out_...  3.29 us
    ppermute x1, starting transfers between devices, body(): pair = pack(cast(source), lax.ppermute(source, 'strip', sibling))  1.42 us
    ppermute x1, starting transfers between devices, body(): follower = lax.ppermute(pair, 'strip', following)  1.37 us
  transfers between devices with their start and end apart: 6, of which 3 were waited for; matrix products, arithmetic and copies ran while one was open for 0% of the time, Pallas kernels for 27%

profile of v3, /device:TPU:1, one launch (start us, length us, event | category | flops | bytes accessed | tf_op | source)
XLA Modules:
  0.0 42.9 jit_solution(7253763006382961401)
XLA Ops:
  0.0 0.0 copy-start.3
  0.0 1.4 %collective-permute-start = (f32[64,512]{1,0:T(8,128)}, f32[64,512]{1,0:T(8,128)S(1)}, u32[]{:S(2)}, u32[]{:S(2)}) collective-permute-start(f32[64,512]{1,0:T(8,128)} %bitcast.6), channel_id=1, source_target_pairs={{0,1},{1,0},{2,3},{3,2},{4,5},{5,4},{6,7},{7,6},{8,9},{9,8},{10,11... | collective-permute-start | bytes 393224 | tf_op jit(solution)/shard_map/ppermute | solution.py:301
  1.4 0.0 copy-start
  1.4 0.9 %copy-done = f32[512,64]{0,1:T(8,128)S(1)} copy-done((f32[512,64]{0,1:T(8,128)S(1)}, f32[512,64]{0,1:T(8,128)}, u32[]{:S(2)}) %copy-start) | copy-done | bytes 131096
  2.3 0.0 copy-start.1
  2.3 0.0 copy-start.2
  2.3 0.3 collective-permute-done.sibling_ref
  2.6 1.4 %collective-permute-start.1 = (bf16[2,64,512]{2,1,0:T(8,128)(2,1)S(1)}, bf16[2,64,512]{2,1,0:T(8,128)(2,1)S(1)}, u32[]{:S(2)}, u32[]{:S(2)}) collective-permute-start(bf16[2,64,512]{2,1,0:T(8,128)(2,1)S(1)} %pack.1.pair_ref), channel_id=1, source_target_pairs={{2,0},{4,2},{6,4},{8,6},{10,8},{12,10},{14,12},{16,14},{18,16},{20... | collective-permute-start | bytes 393224 | tf_op jit(solution)/shard_map/ppermute | solution.py:302
  4.0 3.3 %project.1.raw_ref = bf16[16,128,128]{2,1,0:T(8,128)(2,1)S(1)} custom-call(bf16[2,64,512]{2,1,0:T(8,128)(2,1)S(1)} %pack.1.pair_ref, bf16[512,32,128]{2,1,0:T(8,128)(2,1)} %bitcast.9), custom_call_target="tpu_custom_call" | custom-call | flops 268435456 | bytes 4194304 | tf_op jit(solution)/shard_map/project/pallas_call | solution.py:51
  7.3 0.0 collective-permute-done.1.next_ref
  7.3 0.7 %collective-permute-start.2 = (bf16[2,64,512]{2,1,0:T(8,128)(2,1)S(1)}, bf16[2,64,512]{2,1,0:T(8,128)(2,1)S(1)}, u32[]{:S(2)}, u32[]{:S(2)}) collective-permute-start(bf16[2,64,512]{2,1,0:T(8,128)(2,1)S(1)} %collective-permute-done.1.next_ref), channel_id=1, source_target_pairs={{0,1},{1,0},{2,3},{3,2},{4,5},{5,4},{6,7},{7,6},{8,9},{9,8},{10,11... | collective-permute-start | bytes 393224 | tf_op jit(solution)/shard_map/ppermute | solution.py:305
  8.0 1.0 %order.1 = bf16[128,16,128]{2,1,0:T(8,128)(2,1)} custom-call(bf16[16,128,128]{2,1,0:T(8,128)(2,1)S(1)} %project.1.raw_ref), custom_call_target="tpu_custom_call" | custom-call | bytes 1048576 | tf_op jit(solution)/shard_map/order/pallas_call | solution.py:78
  9.0 0.0 collective-permute-done.2.other_ref
  9.1 4.7 %collective-permute-start.3 = (bf16[6,64,512]{2,1,0:T(8,128)(2,1)S(1)}, bf16[6,64,512]{2,1,0:T(8,128)(2,1)S(1)}, u32[]{:S(2)}, u32[]{:S(2)}) collective-permute-start(bf16[6,64,512]{2,1,0:T(8,128)(2,1)S(1)} %group.1.own_ref), channel_id=1, source_target_pairs={{6,0},{8,2},{10,4},{12,6},{14,8},{16,10},{18,12},{20,14},{22,16},{... | collective-permute-start | bytes 1179656 | tf_op jit(solution)/shard_map/ppermute | solution.py:309
  13.8 10.8 %all-to-all-start = ((bf16[128,16,128]{2,1,0:T(8,128)(2,1)}), bf16[128,16,128]{2,1,0:T(8,128)(2,1)S(1)}, u32[]{:S(2)}, u32[]{:S(2)}) async-start(bf16[128,16,128]{2,1,0:T(8,128)(2,1)} %order.1), calls=%async_computation | async-start | bytes 1048576 | tf_op jit(solution)/shard_map/all_to_all | solution.py:310
  24.7 0.0 collective-permute-done.3.direct_ref
  24.7 1.1 %collective-permute-start.4 = (bf16[6,64,512]{2,1,0:T(8,128)(2,1)S(1)}, bf16[6,64,512]{2,1,0:T(8,128)(2,1)S(1)}, u32[]{:S(2)}, u32[]{:S(2)}) collective-permute-start(bf16[6,64,512]{2,1,0:T(8,128)(2,1)S(1)} %collective-permute-done.3.direct_ref), channel_id=1, source_target_pairs={{0,1},{1,0},{2,3},{3,2},{4,5},{5,4},{6,7},{7,6},{8,9},{9,8},{10,11... | collective-permute-start | bytes 1179656 | tf_op jit(solution)/shard_map/ppermute | solution.py:311
  25.8 1.3 %collective-permute-done.4.swapped_ref = bf16[6,64,512]{2,1,0:T(8,128)(2,1)S(1)} collective-permute-done((bf16[6,64,512]{2,1,0:T(8,128)(2,1)S(1)}, bf16[6,64,512]{2,1,0:T(8,128)(2,1)S(1)}, u32[]{:S(2)}, u32[]{:S(2)}) %collective-permute-start.4) | collective-permute-done | bytes 393248 | tf_op jit(solution)/shard_map/ppermute | solution.py:311
  27.2 0.0 copy-done.3
  27.2 0.0 copy-done.1
  27.2 0.0 copy-done.2
  27.2 7.1 %near.1 = (f32[64,512]{1,0:T(8,128)S(1)}, bf16[128,128]{1,0:T(8,128)(2,1)S(1)}) custom-call(s32[1]{0:T(128)} %bitcast.me_ref, s32[12,128]{1,0:T(8,128)S(1)} %bitcast.8, s32[128]{0:T(128)S(1)} %copy-done.3, f32[512,6144]{1,0:T(8,128)} %blocks_hbm.1, s32[128,128]{1,0:T(8,128)S(1)} %copy-done.1, bf16[6,64,512]{2,1,0:T(8,128)(2,1)S(1)} %group.1.own_ref, ...), custom_call_target="tpu_custom_call" | custom-call | flops 805306368 | bytes 12582912 | tf_op jit(solution)/shard_map/near/pallas_call | solution.py:211
  34.3 4.1 %all-to-all-done.coefficients_ref = bf16[128,16,128]{2,1,0:T(8,128)(2,1)S(1)} async-done(((bf16[128,16,128]{2,1,0:T(8,128)(2,1)}), bf16[128,16,128]{2,1,0:T(8,128)(2,1)S(1)}, u32[]{:S(2)}, u32[]{:S(2)}) %all-to-all-start) | async-done | bytes 524320 | tf_op jit(solution)/shard_map/all_to_all | solution.py:310
  38.4 4.5 %add_far.1 = f32[64,512]{1,0:T(8,128)} custom-call(f32[64,512]{1,0:T(8,128)S(1)} %get-tuple-element.18.near_ref, bf16[128,128]{1,0:T(8,128)(2,1)S(1)} %get-tuple-element.19.rank_ref, bf16[512,32,128]{2,1,0:T(8,128)(2,1)} %bitcast.10, bf16[128,16,128]{2,1,0:T(8,128)(2,1)S(1)} %all-to-all-done.coefficients_ref), custom_call_target="tpu_custom_call" | custom-call | flops 268435456 | bytes 4194304 | tf_op jit(solution)/shard_map/add_far/pallas_call | solution.py:265
  (3 shorter events, 0.1 us)
Async XLA Ops:
  0.0 27.2 %copy-start.3 = (s32[128]{0:T(128)S(1)}, s32[128]{0:T(128)}, u32[]{:S(2)}) copy-start(s32[128]{0:T(128)} %count_ref.1) | copy-start | bytes 1540
  0.0 2.6 %collective-permute-start = (f32[64,512]{1,0:T(8,128)}, f32[64,512]{1,0:T(8,128)S(1)}, u32[]{:S(2)}, u32[]{:S(2)}) collective-permute-start(f32[64,512]{1,0:T(8,128)} %bitcast.6), channel_id=1, source_target_pairs={{0,1},{1,0},{2,3},{3,2},{4,5},{5,4},{6,7},{7,6},{8,9},{9,8},{10,11... | collective-permute-start | bytes 393224 | tf_op jit(solution)/shard_map/ppermute | solution.py:301
  1.4 0.9 %copy-start = (f32[512,64]{0,1:T(8,128)S(1)}, f32[512,64]{0,1:T(8,128)}, u32[]{:S(2)}) copy-start(f32[512,64]{0,1:T(8,128)} %param.7) | copy-start | bytes 393220
  2.3 24.8 %copy-start.1 = (s32[128,128]{1,0:T(8,128)S(1)}, s32[128,128]{1,0:T(8,128)}, u32[]{:S(2)}) copy-start(s32[128,128]{1,0:T(8,128)} %ranks_ref.1) | copy-start | bytes 196612
  2.3 24.8 %copy-start.2 = (s32[128,12]{0,1:T(8,128)S(1)}, s32[128,12]{0,1:T(8,128)}, u32[]{:S(2)}) copy-start(s32[128,12]{0,1:T(8,128)} %param.12) | copy-start | bytes 18436
  2.6 4.7 %collective-permute-start.1 = (bf16[2,64,512]{2,1,0:T(8,128)(2,1)S(1)}, bf16[2,64,512]{2,1,0:T(8,128)(2,1)S(1)}, u32[]{:S(2)}, u32[]{:S(2)}) collective-permute-start(bf16[2,64,512]{2,1,0:T(8,128)(2,1)S(1)} %pack.1.pair_ref), channel_id=1, source_target_pairs={{2,0},{4,2},{6,4},{8,6},{10,8},{12,10},{14,12},{16,14},{18,16},{20... | collective-permute-start | bytes 393224 | tf_op jit(solution)/shard_map/ppermute | solution.py:302
  7.3 1.7 %collective-permute-start.2 = (bf16[2,64,512]{2,1,0:T(8,128)(2,1)S(1)}, bf16[2,64,512]{2,1,0:T(8,128)(2,1)S(1)}, u32[]{:S(2)}, u32[]{:S(2)}) collective-permute-start(bf16[2,64,512]{2,1,0:T(8,128)(2,1)S(1)} %collective-permute-done.1.next_ref), channel_id=1, source_target_pairs={{0,1},{1,0},{2,3},{3,2},{4,5},{5,4},{6,7},{7,6},{8,9},{9,8},{10,11... | collective-permute-start | bytes 393224 | tf_op jit(solution)/shard_map/ppermute | solution.py:305
  9.1 15.6 %collective-permute-start.3 = (bf16[6,64,512]{2,1,0:T(8,128)(2,1)S(1)}, bf16[6,64,512]{2,1,0:T(8,128)(2,1)S(1)}, u32[]{:S(2)}, u32[]{:S(2)}) collective-permute-start(bf16[6,64,512]{2,1,0:T(8,128)(2,1)S(1)} %group.1.own_ref), channel_id=1, source_target_pairs={{6,0},{8,2},{10,4},{12,6},{14,8},{16,10},{18,12},{20,14},{22,16},{... | collective-permute-start | bytes 1179656 | tf_op jit(solution)/shard_map/ppermute | solution.py:309
  13.8 24.6 %all-to-all-start = ((bf16[128,16,128]{2,1,0:T(8,128)(2,1)}), bf16[128,16,128]{2,1,0:T(8,128)(2,1)S(1)}, u32[]{:S(2)}, u32[]{:S(2)}) async-start(bf16[128,16,128]{2,1,0:T(8,128)(2,1)} %order.1), calls=%async_computation | async-start | bytes 1048576 | tf_op jit(solution)/shard_map/all_to_all | solution.py:310
  24.7 2.5 %collective-permute-start.4 = (bf16[6,64,512]{2,1,0:T(8,128)(2,1)S(1)}, bf16[6,64,512]{2,1,0:T(8,128)(2,1)S(1)}, u32[]{:S(2)}, u32[]{:S(2)}) collective-permute-start(bf16[6,64,512]{2,1,0:T(8,128)(2,1)S(1)} %collective-permute-done.3.direct_ref), channel_id=1, source_target_pairs={{0,1},{1,0},{2,3},{3,2},{4,5},{5,4},{6,7},{7,6},{8,9},{9,8},{10,11... | collective-permute-start | bytes 1179656 | tf_op jit(solution)/shard_map/ppermute | solution.py:311

commit v4 on v3

--- a/solution.py
+++ b/solution.py
@@ -232,54 +232,82 @@
     )(me, near_list.T, near_count, near_blocks, ranks, own, direct, swapped)
 
 
-def far_kernel(near_ref, rank_ref, u_hbm, coefficients_ref, out_ref, raw_ref, turned_ref, sems):
-    parts, rows, half, strips = raw_ref.shape
+def turn_kernel(raw_ref, out_ref):
+    out_ref[...] = jnp.swapaxes(raw_ref[...], 0, 1)
+
+
+def turn_half(factors):
+    rows, rank_max, strips = factors.shape
+    half = rank_max // 2
+    return pl.pallas_call(
+        turn_kernel,
+        grid=(1,),
+        in_specs=[pl.BlockSpec((rows, half, strips), lambda i: (0, 0, 0))],
+        out_specs=pl.BlockSpec((half, rows, strips), lambda i: (0, 0, 0)),
+        out_shape=jax.ShapeDtypeStruct((half, rows, strips), bf16),
+        compiler_params=pltpu.CompilerParams(vmem_limit_bytes=16 * MiB),
+        cost_estimate=pl.CostEstimate(
+            flops=0, bytes_accessed=2 * rows * rank_max * strips, transcendentals=0
+        ),
+        name="turn",
+    )(factors)
+
+
+def far_kernel(near_ref, rank_ref, first_ref, u_hbm, coefficients_ref, out_ref, raw_ref, turned_ref, sems):
+    half, rows, strips = first_ref.shape
     sides = out_ref.shape[0]
-    pieces = sems.shape[1]
+    pieces = sems.shape[0]
     chunk = rows // pieces
-    copies = staged_copies(u_hbm, raw_ref, sems)
+    copies = [
+        pltpu.make_async_copy(
+            u_hbm.at[pl.ds(n * chunk, chunk), pl.ds(half, half)],
+            raw_ref.at[pl.ds(n * chunk, chunk)],
+            sems.at[n],
+        )
+        for n in range(pieces)
+    ]
     start_all(copies)
     rank = rank_ref[...]
     turned = jnp.swapaxes(coefficients_ref[...], 0, 1)
     weights = []
-    for p in range(parts * half // 2):
+    for p in range(half):
         kept = jnp.where(rank > 2 * p, turned[p], jnp.zeros_like(turned[p]))
         weights += [kept[:, :sides], kept[:, sides:]]
-    far = jnp.zeros((rows, sides), f32)
-    for h in range(parts):
-        for n in range(pieces):
-            copies[h * pieces + n].wait()
-            part = pl.ds(n * chunk, chunk)
-            turned_ref[h, :, part, :] = jnp.swapaxes(raw_ref[h, part], 0, 1)
-        factors = jnp.concatenate([turned_ref[h, k] for k in range(half)], axis=1)
-        part = jnp.concatenate(weights[h * half : (h + 1) * half], axis=0)
-        far += jnp.dot(factors, part, preferred_element_type=f32)
+    factors = jnp.concatenate([first_ref[k] for k in range(half)], axis=1)
+    part = jnp.concatenate(weights[:half], axis=0)
+    far = jnp.dot(factors, part, preferred_element_type=f32)
+    for n in range(pieces):
+        copies[n].wait()
+        part = pl.ds(n * chunk, chunk)
+        turned_ref[:, part, :] = jnp.swapaxes(raw_ref[part], 0, 1)
+    factors = jnp.concatenate([turned_ref[k] for k in range(half)], axis=1)
+    part = jnp.concatenate(weights[half:], axis=0)
+    far += jnp.dot(factors, part, preferred_element_type=f32)
     out_ref[...] = near_ref[...] + far.T
 
 
-def add_far(near_field, rank, u_far, coefficients):
+def add_far(near_field, rank, first, u_far, coefficients):
     rows, rank_max, strips = u_far.shape
     sides = near_field.shape[0]
-    parts = 2
-    half = rank_max // parts
+    half = rank_max // 2
     return pl.pallas_call(
         far_kernel,
-        in_specs=[VMEM, VMEM, HBM, VMEM],
+        in_specs=[VMEM, VMEM, VMEM, HBM, VMEM],
         out_specs=VMEM,
         out_shape=jax.ShapeDtypeStruct((sides, rows), f32),
         scratch_shapes=[
-            pltpu.VMEM((parts, rows, half, strips), bf16),
-            pltpu.VMEM((parts, half, rows, strips), bf16),
-            pltpu.SemaphoreType.DMA((parts, 4)),
+            pltpu.VMEM((rows, half, strips), bf16),
+            pltpu.VMEM((half, rows, strips), bf16),
+            pltpu.SemaphoreType.DMA((8,)),
         ],
-        compiler_params=pltpu.CompilerParams(vmem_limit_bytes=53 * MiB),
+        compiler_params=pltpu.CompilerParams(vmem_limit_bytes=51 * MiB),
         cost_estimate=pl.CostEstimate(
             flops=2 * rows * rank_max * strips * sides,
             bytes_accessed=2 * rows * rank_max * strips,
             transcendentals=0,
         ),
         name="add_far",
-    )(near_field, rank, u_far, coefficients)
+    )(near_field, rank, first, u_far, coefficients)
 
 
 def exchanges(strips):
@@ -310,7 +338,8 @@
     incoming = lax.all_to_all(outgoing, "strip", split_axis=0, concat_axis=0, tiled=True)
     swapped = lax.ppermute(direct, "strip", sibling)
     near_field, rank = near(me, near_list, near_count, near_blocks, ranks, own, direct, swapped)
-    return add_far(near_field, rank, jnp.transpose(u_far, (0, 2, 1)), incoming).T
+    u_far, near_field = lax.optimization_barrier((jnp.transpose(u_far, (0, 2, 1)), near_field))
+    return add_far(near_field, rank, turn_half(u_far), u_far, incoming).T
 
 
 def solution(mesh):

time: 43.1 us -> 42.3 us (0.981)
  waiting for transfers between devices: 5.72 us -> 4.5 us
    all_to_all x1, waiting for transfers between devices: 4.08 us -> 2.86 us  [body(): lax.all_to_all(outgoing, 'strip', split_axis=0, concat_axis=0, tiled=True)]
    pallas_call x1 -> x2, Pallas kernels: 4.51 us -> 4.79 us  [the longest x1 3.76 us: add_far(): pl.pallas_call(far_kernel, in_specs=[VMEM, VMEM, VMEM, HBM, VMEM], out_sp...]
    unnamed x8 -> x10, local copies, waits for them, and re-layouts: 0.91 us -> 0.92 us
  transfers between devices with their start and end apart: 6 -> 6, of which waited for: 3 -> 3; matrix products, arithmetic and copies ran while one was open for 0% -> 0% of each run, Pallas kernels for 27% -> 30%
where the time goes in v4:
time: 42.3 us; the launch traced here: 42.1 us
  starting transfers between devices  20.2 us (48%)
  Pallas kernels  16.4 us (39%)
  waiting for transfers between devices  4.5 us (11%)
  local copies, waits for them, and re-layouts  0.92 us (2%)
    all_to_all x1, starting transfers between devices, body(): lax.all_to_all(outgoing, 'strip', split_axis=0, concat_axis=0, tiled=True)  10.8 us
    pallas_call x1, Pallas kernels, near(): pl.pallas_call(near_kernel, in_specs=[SMEM, SMEM, SMEM, HBM, VMEM, VMEM,...  7.29 us
    ppermute x1, starting transfers between devices, body(): direct = lax.ppermute(own, 'strip', groups)  4.75 us
    pallas_call x1, Pallas kernels, add_far(): pl.pallas_call(far_kernel, in_specs=[VMEM, VMEM, VMEM, HBM, VMEM], out_sp...  3.76 us
    pallas_call x1, Pallas kernels, project(): pl.pallas_call(project_kernel, in_specs=[VMEM, HBM], out_specs=VMEM, out_...  3.29 us
    all_to_all x1, waiting for transfers between devices, body(): lax.all_to_all(outgoing, 'strip', split_axis=0, concat_axis=0, tiled=True)  2.86 us
    ppermute x1, starting transfers between devices, body(): pair = pack(cast(source), lax.ppermute(source, 'strip', sibling))  1.42 us
    ppermute x1, starting transfers between devices, body(): follower = lax.ppermute(pair, 'strip', following)  1.37 us
  transfers between devices with their start and end apart: 6, of which 3 were waited for; matrix products, arithmetic and copies ran while one was open for 0% of the time, Pallas kernels for 30%

profile of v4, /device:TPU:1, one launch (start us, length us, event | category | flops | bytes accessed | tf_op | source)
XLA Modules:
  0.0 42.1 jit_solution(3096188493811366739)
XLA Ops:
  0.0 0.0 copy-start.4
  0.0 1.4 %collective-permute-start = (f32[64,512]{1,0:T(8,128)}, f32[64,512]{1,0:T(8,128)S(1)}, u32[]{:S(2)}, u32[]{:S(2)}) collective-permute-start(f32[64,512]{1,0:T(8,128)} %bitcast.8), channel_id=1, source_target_pairs={{0,1},{1,0},{2,3},{3,2},{4,5},{5,4},{6,7},{7,6},{8,9},{9,8},{10,11... | collective-permute-start | bytes 393224 | tf_op jit(solution)/shard_map/ppermute | solution.py:329
  1.4 0.0 copy-start.1
  1.4 0.9 %copy-done.1 = f32[512,64]{0,1:T(8,128)S(1)} copy-done((f32[512,64]{0,1:T(8,128)S(1)}, f32[512,64]{0,1:T(8,128)}, u32[]{:S(2)}) %copy-start.1) | copy-done | bytes 131096
  2.3 0.0 copy-start.2
  2.3 0.0 copy-start.3
  2.3 0.3 collective-permute-done.sibling_ref
  2.6 1.4 %collective-permute-start.1 = (bf16[2,64,512]{2,1,0:T(8,128)(2,1)S(1)}, bf16[2,64,512]{2,1,0:T(8,128)(2,1)S(1)}, u32[]{:S(2)}, u32[]{:S(2)}) collective-permute-start(bf16[2,64,512]{2,1,0:T(8,128)(2,1)S(1)} %pack.1.pair_ref), channel_id=1, source_target_pairs={{2,0},{4,2},{6,4},{8,6},{10,8},{12,10},{14,12},{16,14},{18,16},{20... | collective-permute-start | bytes 393224 | tf_op jit(solution)/shard_map/ppermute | solution.py:330
  4.0 3.3 %project.1.raw_ref = bf16[16,128,128]{2,1,0:T(8,128)(2,1)S(1)} custom-call(bf16[2,64,512]{2,1,0:T(8,128)(2,1)S(1)} %pack.1.pair_ref, bf16[512,32,128]{2,1,0:T(8,128)(2,1)} %bitcast.11), custom_call_target="tpu_custom_call" | custom-call | flops 268435456 | bytes 4194304 | tf_op jit(solution)/shard_map/project/pallas_call | solution.py:51
  7.3 0.0 collective-permute-done.1.next_ref
  7.3 0.7 %collective-permute-start.2 = (bf16[2,64,512]{2,1,0:T(8,128)(2,1)S(1)}, bf16[2,64,512]{2,1,0:T(8,128)(2,1)S(1)}, u32[]{:S(2)}, u32[]{:S(2)}) collective-permute-start(bf16[2,64,512]{2,1,0:T(8,128)(2,1)S(1)} %collective-permute-done.1.next_ref), channel_id=1, source_target_pairs={{0,1},{1,0},{2,3},{3,2},{4,5},{5,4},{6,7},{7,6},{8,9},{9,8},{10,11... | collective-permute-start | bytes 393224 | tf_op jit(solution)/shard_map/ppermute | solution.py:333
  8.0 1.0 %order.1 = bf16[128,16,128]{2,1,0:T(8,128)(2,1)} custom-call(bf16[16,128,128]{2,1,0:T(8,128)(2,1)S(1)} %project.1.raw_ref), custom_call_target="tpu_custom_call" | custom-call | bytes 1048576 | tf_op jit(solution)/shard_map/order/pallas_call | solution.py:78
  9.1 0.0 collective-permute-done.2.other_ref
  9.1 4.7 %collective-permute-start.3 = (bf16[6,64,512]{2,1,0:T(8,128)(2,1)S(1)}, bf16[6,64,512]{2,1,0:T(8,128)(2,1)S(1)}, u32[]{:S(2)}, u32[]{:S(2)}) collective-permute-start(bf16[6,64,512]{2,1,0:T(8,128)(2,1)S(1)} %group.1.own_ref), channel_id=1, source_target_pairs={{6,0},{8,2},{10,4},{12,6},{14,8},{16,10},{18,12},{20,14},{22,16},{... | collective-permute-start | bytes 1179656 | tf_op jit(solution)/shard_map/ppermute | solution.py:337
  13.8 10.8 %all-to-all-start = ((bf16[128,16,128]{2,1,0:T(8,128)(2,1)}), bf16[128,16,128]{2,1,0:T(8,128)(2,1)S(1)}, u32[]{:S(2)}, u32[]{:S(2)}) async-start(bf16[128,16,128]{2,1,0:T(8,128)(2,1)} %order.1), calls=%async_computation | async-start | bytes 1048576 | tf_op jit(solution)/shard_map/all_to_all | solution.py:338
  24.7 0.0 collective-permute-done.3.direct_ref
  24.7 1.1 %collective-permute-start.4 = (bf16[6,64,512]{2,1,0:T(8,128)(2,1)S(1)}, bf16[6,64,512]{2,1,0:T(8,128)(2,1)S(1)}, u32[]{:S(2)}, u32[]{:S(2)}) collective-permute-start(bf16[6,64,512]{2,1,0:T(8,128)(2,1)S(1)} %collective-permute-done.3.direct_ref), channel_id=1, source_target_pairs={{0,1},{1,0},{2,3},{3,2},{4,5},{5,4},{6,7},{7,6},{8,9},{9,8},{10,11... | collective-permute-start | bytes 1179656 | tf_op jit(solution)/shard_map/ppermute | solution.py:339
  25.8 1.3 %collective-permute-done.4.swapped_ref = bf16[6,64,512]{2,1,0:T(8,128)(2,1)S(1)} collective-permute-done((bf16[6,64,512]{2,1,0:T(8,128)(2,1)S(1)}, bf16[6,64,512]{2,1,0:T(8,128)(2,1)S(1)}, u32[]{:S(2)}, u32[]{:S(2)}) %collective-permute-start.4) | collective-permute-done | bytes 393248 | tf_op jit(solution)/shard_map/ppermute | solution.py:339
  27.2 0.0 copy-done.4
  27.2 0.0 copy-done.2
  27.2 0.0 copy-done.3
  27.2 0.0 copy-start
  27.2 7.3 %near.1 = (f32[64,512]{1,0:T(8,128)S(1)}, bf16[128,128]{1,0:T(8,128)(2,1)S(1)}) custom-call(s32[1]{0:T(128)} %bitcast.1.me_ref, s32[12,128]{1,0:T(8,128)S(1)} %bitcast.10, s32[128]{0:T(128)S(1)} %copy-done.4, f32[512,6144]{1,0:T(8,128)} %blocks_hbm.1, s32[128,128]{1,0:T(8,128)S(1)} %copy-done.2, bf16[6,64,512]{2,1,0:T(8,128)(2,1)S(1)} %group.1.own_ref, ...), custom_call_target="tpu_custom_call" | custom-call | flops 805306368 | bytes 12582912 | tf_op jit(solution)/shard_map/near/pallas_call | solution.py:211
  34.5 0.0 copy-done
  34.5 1.0 %turn.1.first_ref = bf16[16,512,128]{2,1,0:T(8,128)(2,1)S(1)} custom-call(bf16[512,32,128]{2,1,0:T(8,128)(2,1)S(1)} %bitcast.7), custom_call_target="tpu_custom_call" | custom-call | bytes 4194304 | tf_op jit(solution)/shard_map/turn/pallas_call | solution.py:242
  35.5 2.9 %all-to-all-done.coefficients_ref = bf16[128,16,128]{2,1,0:T(8,128)(2,1)S(1)} async-done(((bf16[128,16,128]{2,1,0:T(8,128)(2,1)}), bf16[128,16,128]{2,1,0:T(8,128)(2,1)S(1)}, u32[]{:S(2)}, u32[]{:S(2)}) %all-to-all-start) | async-done | bytes 524320 | tf_op jit(solution)/shard_map/all_to_all | solution.py:338
  38.4 3.8 %add_far.1 = f32[64,512]{1,0:T(8,128)} custom-call(f32[64,512]{1,0:T(8,128)S(1)} %get-tuple-element.21.near_ref, bf16[128,128]{1,0:T(8,128)(2,1)S(1)} %get-tuple-element.22.rank_ref, bf16[16,512,128]{2,1,0:T(8,128)(2,1)S(1)} %turn.1.first_ref, bf16[512,32,128]{2,1,0:T(8,128)(2,1)} %bitcast.6, bf16[128,16,128]{2,1,0:T(8,128)(2,1)S(1)} %all-to-all-done.coefficients_ref), custom_call_target="tpu_custom_call" | custom-call | flops 268435456 | bytes 4194304 | tf_op jit(solution)/shard_map/add_far/pallas_call | solution.py:293
  (3 shorter events, 0.1 us)
Async XLA Ops:
  0.0 27.2 %copy-start.4 = (s32[128]{0:T(128)S(1)}, s32[128]{0:T(128)}, u32[]{:S(2)}) copy-start(s32[128]{0:T(128)} %count_ref.1) | copy-start | bytes 1540
  0.0 2.6 %collective-permute-start = (f32[64,512]{1,0:T(8,128)}, f32[64,512]{1,0:T(8,128)S(1)}, u32[]{:S(2)}, u32[]{:S(2)}) collective-permute-start(f32[64,512]{1,0:T(8,128)} %bitcast.8), channel_id=1, source_target_pairs={{0,1},{1,0},{2,3},{3,2},{4,5},{5,4},{6,7},{7,6},{8,9},{9,8},{10,11... | collective-permute-start | bytes 393224 | tf_op jit(solution)/shard_map/ppermute | solution.py:329
  1.4 0.9 %copy-start.1 = (f32[512,64]{0,1:T(8,128)S(1)}, f32[512,64]{0,1:T(8,128)}, u32[]{:S(2)}) copy-start(f32[512,64]{0,1:T(8,128)} %param.7) | copy-start | bytes 393220
  2.3 24.8 %copy-start.2 = (s32[128,128]{1,0:T(8,128)S(1)}, s32[128,128]{1,0:T(8,128)}, u32[]{:S(2)}) copy-start(s32[128,128]{1,0:T(8,128)} %ranks_ref.1) | copy-start | bytes 196612
  2.3 24.8 %copy-start.3 = (s32[128,12]{0,1:T(8,128)S(1)}, s32[128,12]{0,1:T(8,128)}, u32[]{:S(2)}) copy-start(s32[128,12]{0,1:T(8,128)} %param.12) | copy-start | bytes 18436
  2.6 4.7 %collective-permute-start.1 = (bf16[2,64,512]{2,1,0:T(8,128)(2,1)S(1)}, bf16[2,64,512]{2,1,0:T(8,128)(2,1)S(1)}, u32[]{:S(2)}, u32[]{:S(2)}) collective-permute-start(bf16[2,64,512]{2,1,0:T(8,128)(2,1)S(1)} %pack.1.pair_ref), channel_id=1, source_target_pairs={{2,0},{4,2},{6,4},{8,6},{10,8},{12,10},{14,12},{16,14},{18,16},{20... | collective-permute-start | bytes 393224 | tf_op jit(solution)/shard_map/ppermute | solution.py:330
  7.3 1.7 %collective-permute-start.2 = (bf16[2,64,512]{2,1,0:T(8,128)(2,1)S(1)}, bf16[2,64,512]{2,1,0:T(8,128)(2,1)S(1)}, u32[]{:S(2)}, u32[]{:S(2)}) collective-permute-start(bf16[2,64,512]{2,1,0:T(8,128)(2,1)S(1)} %collective-permute-done.1.next_ref), channel_id=1, source_target_pairs={{0,1},{1,0},{2,3},{3,2},{4,5},{5,4},{6,7},{7,6},{8,9},{9,8},{10,11... | collective-permute-start | bytes 393224 | tf_op jit(solution)/shard_map/ppermute | solution.py:333
  9.1 15.6 %collective-permute-start.3 = (bf16[6,64,512]{2,1,0:T(8,128)(2,1)S(1)}, bf16[6,64,512]{2,1,0:T(8,128)(2,1)S(1)}, u32[]{:S(2)}, u32[]{:S(2)}) collective-permute-start(bf16[6,64,512]{2,1,0:T(8,128)(2,1)S(1)} %group.1.own_ref), channel_id=1, source_target_pairs={{6,0},{8,2},{10,4},{12,6},{14,8},{16,10},{18,12},{20,14},{22,16},{... | collective-permute-start | bytes 1179656 | tf_op jit(solution)/shard_map/ppermute | solution.py:337
  13.8 24.5 %all-to-all-start = ((bf16[128,16,128]{2,1,0:T(8,128)(2,1)}), bf16[128,16,128]{2,1,0:T(8,128)(2,1)S(1)}, u32[]{:S(2)}, u32[]{:S(2)}) async-start(bf16[128,16,128]{2,1,0:T(8,128)(2,1)} %order.1), calls=%async_computation | async-start | bytes 1048576 | tf_op jit(solution)/shard_map/all_to_all | solution.py:338
  24.7 2.5 %collective-permute-start.4 = (bf16[6,64,512]{2,1,0:T(8,128)(2,1)S(1)}, bf16[6,64,512]{2,1,0:T(8,128)(2,1)S(1)}, u32[]{:S(2)}, u32[]{:S(2)}) collective-permute-start(bf16[6,64,512]{2,1,0:T(8,128)(2,1)S(1)} %collective-permute-done.3.direct_ref), channel_id=1, source_target_pairs={{0,1},{1,0},{2,3},{3,2},{4,5},{5,4},{6,7},{7,6},{8,9},{9,8},{10,11... | collective-permute-start | bytes 1179656 | tf_op jit(solution)/shard_map/ppermute | solution.py:339
  27.2 7.3 %copy-start = (bf16[512,128,32]{1,2,0:T(8,128)(2,1)S(1)}, bf16[512,128,32]{1,2,0:T(8,128)(2,1)}, u32[]{:S(2)}) copy-start(bf16[512,128,32]{1,2,0:T(8,128)(2,1)} %param.9) | copy-start | bytes 12582916

commit v5 on v4

--- a/solution.py
+++ b/solution.py
@@ -56,7 +56,7 @@
         scratch_shapes=[
             pltpu.VMEM((parts, rows, rank_max // parts, strips), bf16),
             pltpu.VMEM((rank_max, rows, strips), bf16),
-            pltpu.SemaphoreType.DMA((parts, 4)),
+            pltpu.SemaphoreType.DMA((parts, 8)),
         ],
         compiler_params=pltpu.CompilerParams(vmem_limit_bytes=53 * MiB),
         cost_estimate=pl.CostEstimate(

time: 42.3 us -> 42.3 us (level)
  no operation moved by 1% of the time
where the time goes in v5:
time: 42.3 us; the launch traced here: 42.1 us
  starting transfers between devices  20.2 us (48%)
  Pallas kernels  16.5 us (39%)
  waiting for transfers between devices  4.5 us (11%)
  local copies, waits for them, and re-layouts  0.92 us (2%)
    all_to_all x1, starting transfers between devices, body(): lax.all_to_all(outgoing, 'strip', split_axis=0, concat_axis=0, tiled=True)  10.8 us
    pallas_call x1, Pallas kernels, near(): pl.pallas_call(near_kernel, in_specs=[SMEM, SMEM, SMEM, HBM, VMEM, VMEM,...  7.29 us
    ppermute x1, starting transfers between devices, body(): direct = lax.ppermute(own, 'strip', groups)  4.75 us
    pallas_call x1, Pallas kernels, add_far(): pl.pallas_call(far_kernel, in_specs=[VMEM, VMEM, VMEM, HBM, VMEM], out_sp...  3.76 us
    pallas_call x1, Pallas kernels, project(): pl.pallas_call(project_kernel, in_specs=[VMEM, HBM], out_specs=VMEM, out_...  3.33 us
    all_to_all x1, waiting for transfers between devices, body(): lax.all_to_all(outgoing, 'strip', split_axis=0, concat_axis=0, tiled=True)  2.86 us
    ppermute x1, starting transfers between devices, body(): pair = pack(cast(source), lax.ppermute(source, 'strip', sibling))  1.42 us
    ppermute x1, starting transfers between devices, body(): follower = lax.ppermute(pair, 'strip', following)  1.37 us
  transfers between devices with their start and end apart: 6, of which 3 were waited for; matrix products, arithmetic and copies ran while one was open for 0% of the time, Pallas kernels for 30%

profile of v5, /device:TPU:1, one launch (start us, length us, event | category | flops | bytes accessed | tf_op | source)
XLA Modules:
  0.0 42.1 jit_solution(5523622253140791830)
XLA Ops:
  0.0 0.0 copy-start.4
  0.0 1.4 %collective-permute-start = (f32[64,512]{1,0:T(8,128)}, f32[64,512]{1,0:T(8,128)S(1)}, u32[]{:S(2)}, u32[]{:S(2)}) collective-permute-start(f32[64,512]{1,0:T(8,128)} %bitcast.8), channel_id=1, source_target_pairs={{0,1},{1,0},{2,3},{3,2},{4,5},{5,4},{6,7},{7,6},{8,9},{9,8},{10,11... | collective-permute-start | bytes 393224 | tf_op jit(solution)/shard_map/ppermute | solution.py:329
  1.4 0.0 copy-start.1
  1.4 0.9 %copy-done.1 = f32[512,64]{0,1:T(8,128)S(1)} copy-done((f32[512,64]{0,1:T(8,128)S(1)}, f32[512,64]{0,1:T(8,128)}, u32[]{:S(2)}) %copy-start.1) | copy-done | bytes 131096
  2.3 0.0 copy-start.2
  2.3 0.0 copy-start.3
  2.3 0.3 collective-permute-done.sibling_ref
  2.6 1.4 %collective-permute-start.1 = (bf16[2,64,512]{2,1,0:T(8,128)(2,1)S(1)}, bf16[2,64,512]{2,1,0:T(8,128)(2,1)S(1)}, u32[]{:S(2)}, u32[]{:S(2)}) collective-permute-start(bf16[2,64,512]{2,1,0:T(8,128)(2,1)S(1)} %pack.1.pair_ref), channel_id=1, source_target_pairs={{2,0},{4,2},{6,4},{8,6},{10,8},{12,10},{14,12},{16,14},{18,16},{20... | collective-permute-start | bytes 393224 | tf_op jit(solution)/shard_map/ppermute | solution.py:330
  4.0 3.3 %project.1.raw_ref = bf16[16,128,128]{2,1,0:T(8,128)(2,1)S(1)} custom-call(bf16[2,64,512]{2,1,0:T(8,128)(2,1)S(1)} %pack.1.pair_ref, bf16[512,32,128]{2,1,0:T(8,128)(2,1)} %bitcast.11), custom_call_target="tpu_custom_call" | custom-call | flops 268435456 | bytes 4194304 | tf_op jit(solution)/shard_map/project/pallas_call | solution.py:51
  7.3 0.0 collective-permute-done.1.next_ref
  7.4 0.7 %collective-permute-start.2 = (bf16[2,64,512]{2,1,0:T(8,128)(2,1)S(1)}, bf16[2,64,512]{2,1,0:T(8,128)(2,1)S(1)}, u32[]{:S(2)}, u32[]{:S(2)}) collective-permute-start(bf16[2,64,512]{2,1,0:T(8,128)(2,1)S(1)} %collective-permute-done.1.next_ref), channel_id=1, source_target_pairs={{0,1},{1,0},{2,3},{3,2},{4,5},{5,4},{6,7},{7,6},{8,9},{9,8},{10,11... | collective-permute-start | bytes 393224 | tf_op jit(solution)/shard_map/ppermute | solution.py:333
  8.0 1.0 %order.1 = bf16[128,16,128]{2,1,0:T(8,128)(2,1)} custom-call(bf16[16,128,128]{2,1,0:T(8,128)(2,1)S(1)} %project.1.raw_ref), custom_call_target="tpu_custom_call" | custom-call | bytes 1048576 | tf_op jit(solution)/shard_map/order/pallas_call | solution.py:78
  9.1 0.0 collective-permute-done.2.other_ref
  9.1 4.7 %collective-permute-start.3 = (bf16[6,64,512]{2,1,0:T(8,128)(2,1)S(1)}, bf16[6,64,512]{2,1,0:T(8,128)(2,1)S(1)}, u32[]{:S(2)}, u32[]{:S(2)}) collective-permute-start(bf16[6,64,512]{2,1,0:T(8,128)(2,1)S(1)} %group.1.own_ref), channel_id=1, source_target_pairs={{6,0},{8,2},{10,4},{12,6},{14,8},{16,10},{18,12},{20,14},{22,16},{... | collective-permute-start | bytes 1179656 | tf_op jit(solution)/shard_map/ppermute | solution.py:337
  13.8 10.8 %all-to-all-start = ((bf16[128,16,128]{2,1,0:T(8,128)(2,1)}), bf16[128,16,128]{2,1,0:T(8,128)(2,1)S(1)}, u32[]{:S(2)}, u32[]{:S(2)}) async-start(bf16[128,16,128]{2,1,0:T(8,128)(2,1)} %order.1), calls=%async_computation | async-start | bytes 1048576 | tf_op jit(solution)/shard_map/all_to_all | solution.py:338
  24.7 0.0 collective-permute-done.3.direct_ref
  24.7 1.1 %collective-permute-start.4 = (bf16[6,64,512]{2,1,0:T(8,128)(2,1)S(1)}, bf16[6,64,512]{2,1,0:T(8,128)(2,1)S(1)}, u32[]{:S(2)}, u32[]{:S(2)}) collective-permute-start(bf16[6,64,512]{2,1,0:T(8,128)(2,1)S(1)} %collective-permute-done.3.direct_ref), channel_id=1, source_target_pairs={{0,1},{1,0},{2,3},{3,2},{4,5},{5,4},{6,7},{7,6},{8,9},{9,8},{10,11... | collective-permute-start | bytes 1179656 | tf_op jit(solution)/shard_map/ppermute | solution.py:339
  25.8 1.3 %collective-permute-done.4.swapped_ref = bf16[6,64,512]{2,1,0:T(8,128)(2,1)S(1)} collective-permute-done((bf16[6,64,512]{2,1,0:T(8,128)(2,1)S(1)}, bf16[6,64,512]{2,1,0:T(8,128)(2,1)S(1)}, u32[]{:S(2)}, u32[]{:S(2)}) %collective-permute-start.4) | collective-permute-done | bytes 393248 | tf_op jit(solution)/shard_map/ppermute | solution.py:339
  27.2 0.0 copy-done.4
  27.2 0.0 copy-done.2
  27.2 0.0 copy-done.3
  27.2 0.0 copy-start
  27.2 7.3 %near.1 = (f32[64,512]{1,0:T(8,128)S(1)}, bf16[128,128]{1,0:T(8,128)(2,1)S(1)}) custom-call(s32[1]{0:T(128)} %bitcast.1.me_ref, s32[12,128]{1,0:T(8,128)S(1)} %bitcast.10, s32[128]{0:T(128)S(1)} %copy-done.4, f32[512,6144]{1,0:T(8,128)} %blocks_hbm.1, s32[128,128]{1,0:T(8,128)S(1)} %copy-done.2, bf16[6,64,512]{2,1,0:T(8,128)(2,1)S(1)} %group.1.own_ref, ...), custom_call_target="tpu_custom_call" | custom-call | flops 805306368 | bytes 12582912 | tf_op jit(solution)/shard_map/near/pallas_call | solution.py:211
  34.5 0.0 copy-done
  34.5 1.0 %turn.1.first_ref = bf16[16,512,128]{2,1,0:T(8,128)(2,1)S(1)} custom-call(bf16[512,32,128]{2,1,0:T(8,128)(2,1)S(1)} %bitcast.7), custom_call_target="tpu_custom_call" | custom-call | bytes 4194304 | tf_op jit(solution)/shard_map/turn/pallas_call | solution.py:242
  35.5 2.9 %all-to-all-done.coefficients_ref = bf16[128,16,128]{2,1,0:T(8,128)(2,1)S(1)} async-done(((bf16[128,16,128]{2,1,0:T(8,128)(2,1)}), bf16[128,16,128]{2,1,0:T(8,128)(2,1)S(1)}, u32[]{:S(2)}, u32[]{:S(2)}) %all-to-all-start) | async-done | bytes 524320 | tf_op jit(solution)/shard_map/all_to_all | solution.py:338
  38.4 3.8 %add_far.1 = f32[64,512]{1,0:T(8,128)} custom-call(f32[64,512]{1,0:T(8,128)S(1)} %get-tuple-element.21.near_ref, bf16[128,128]{1,0:T(8,128)(2,1)S(1)} %get-tuple-element.22.rank_ref, bf16[16,512,128]{2,1,0:T(8,128)(2,1)S(1)} %turn.1.first_ref, bf16[512,32,128]{2,1,0:T(8,128)(2,1)} %bitcast.6, bf16[128,16,128]{2,1,0:T(8,128)(2,1)S(1)} %all-to-all-done.coefficients_ref), custom_call_target="tpu_custom_call" | custom-call | flops 268435456 | bytes 4194304 | tf_op jit(solution)/shard_map/add_far/pallas_call | solution.py:293
  (3 shorter events, 0.1 us)
Async XLA Ops:
  0.0 27.2 %copy-start.4 = (s32[128]{0:T(128)S(1)}, s32[128]{0:T(128)}, u32[]{:S(2)}) copy-start(s32[128]{0:T(128)} %count_ref.1) | copy-start | bytes 1540
  0.0 2.6 %collective-permute-start = (f32[64,512]{1,0:T(8,128)}, f32[64,512]{1,0:T(8,128)S(1)}, u32[]{:S(2)}, u32[]{:S(2)}) collective-permute-start(f32[64,512]{1,0:T(8,128)} %bitcast.8), channel_id=1, source_target_pairs={{0,1},{1,0},{2,3},{3,2},{4,5},{5,4},{6,7},{7,6},{8,9},{9,8},{10,11... | collective-permute-start | bytes 393224 | tf_op jit(solution)/shard_map/ppermute | solution.py:329
  1.4 0.9 %copy-start.1 = (f32[512,64]{0,1:T(8,128)S(1)}, f32[512,64]{0,1:T(8,128)}, u32[]{:S(2)}) copy-start(f32[512,64]{0,1:T(8,128)} %param.7) | copy-start | bytes 393220
  2.3 24.8 %copy-start.2 = (s32[128,128]{1,0:T(8,128)S(1)}, s32[128,128]{1,0:T(8,128)}, u32[]{:S(2)}) copy-start(s32[128,128]{1,0:T(8,128)} %ranks_ref.1) | copy-start | bytes 196612
  2.3 24.8 %copy-start.3 = (s32[128,12]{0,1:T(8,128)S(1)}, s32[128,12]{0,1:T(8,128)}, u32[]{:S(2)}) copy-start(s32[128,12]{0,1:T(8,128)} %param.12) | copy-start | bytes 18436
  2.6 4.7 %collective-permute-start.1 = (bf16[2,64,512]{2,1,0:T(8,128)(2,1)S(1)}, bf16[2,64,512]{2,1,0:T(8,128)(2,1)S(1)}, u32[]{:S(2)}, u32[]{:S(2)}) collective-permute-start(bf16[2,64,512]{2,1,0:T(8,128)(2,1)S(1)} %pack.1.pair_ref), channel_id=1, source_target_pairs={{2,0},{4,2},{6,4},{8,6},{10,8},{12,10},{14,12},{16,14},{18,16},{20... | collective-permute-start | bytes 393224 | tf_op jit(solution)/shard_map/ppermute | solution.py:330
  7.4 1.7 %collective-permute-start.2 = (bf16[2,64,512]{2,1,0:T(8,128)(2,1)S(1)}, bf16[2,64,512]{2,1,0:T(8,128)(2,1)S(1)}, u32[]{:S(2)}, u32[]{:S(2)}) collective-permute-start(bf16[2,64,512]{2,1,0:T(8,128)(2,1)S(1)} %collective-permute-done.1.next_ref), channel_id=1, source_target_pairs={{0,1},{1,0},{2,3},{3,2},{4,5},{5,4},{6,7},{7,6},{8,9},{9,8},{10,11... | collective-permute-start | bytes 393224 | tf_op jit(solution)/shard_map/ppermute | solution.py:333
  9.1 15.6 %collective-permute-start.3 = (bf16[6,64,512]{2,1,0:T(8,128)(2,1)S(1)}, bf16[6,64,512]{2,1,0:T(8,128)(2,1)S(1)}, u32[]{:S(2)}, u32[]{:S(2)}) collective-permute-start(bf16[6,64,512]{2,1,0:T(8,128)(2,1)S(1)} %group.1.own_ref), channel_id=1, source_target_pairs={{6,0},{8,2},{10,4},{12,6},{14,8},{16,10},{18,12},{20,14},{22,16},{... | collective-permute-start | bytes 1179656 | tf_op jit(solution)/shard_map/ppermute | solution.py:337
  13.8 24.5 %all-to-all-start = ((bf16[128,16,128]{2,1,0:T(8,128)(2,1)}), bf16[128,16,128]{2,1,0:T(8,128)(2,1)S(1)}, u32[]{:S(2)}, u32[]{:S(2)}) async-start(bf16[128,16,128]{2,1,0:T(8,128)(2,1)} %order.1), calls=%async_computation | async-start | bytes 1048576 | tf_op jit(solution)/shard_map/all_to_all | solution.py:338
  24.7 2.5 %collective-permute-start.4 = (bf16[6,64,512]{2,1,0:T(8,128)(2,1)S(1)}, bf16[6,64,512]{2,1,0:T(8,128)(2,1)S(1)}, u32[]{:S(2)}, u32[]{:S(2)}) collective-permute-start(bf16[6,64,512]{2,1,0:T(8,128)(2,1)S(1)} %collective-permute-done.3.direct_ref), channel_id=1, source_target_pairs={{0,1},{1,0},{2,3},{3,2},{4,5},{5,4},{6,7},{7,6},{8,9},{9,8},{10,11... | collective-permute-start | bytes 1179656 | tf_op jit(solution)/shard_map/ppermute | solution.py:339
  27.2 7.3 %copy-start = (bf16[512,128,32]{1,2,0:T(8,128)(2,1)S(1)}, bf16[512,128,32]{1,2,0:T(8,128)(2,1)}, u32[]{:S(2)}) copy-start(bf16[512,128,32]{1,2,0:T(8,128)(2,1)} %param.9) | copy-start | bytes 12582916
